TPU v7x, 32 devices: a whole 2x2x4 slice. The times are simulated.
32 devices in a mesh: rep: 2 (over y), ep: 16 (over z, x, core).
Axes of the slice: x: 2, y: 2, z: 4, core: 2. Of those that a mesh axis runs over, the one named last changes fastest.
Arguments:
- signal: bfloat16 [2048, 4096], P('ep', 'rep'), may hold values from -6 to 6
- routes: int32 [2048, 8], P('ep'), may hold values from 0 to 15, all different within a row; in each aligned block of 128 rows (0 to 127, 128 to 255, ...) at most 80 rows name the same one
- gates: float32 [2048, 8], P('ep'), may hold values from 0.05 to 0.5
- pairing: int32 [1536], P('ep'), may hold values from 0 to 31
- w_gate: bfloat16 [16, 4096, 768], P('ep', 'rep'), may hold values from -0.09375 to 0.09375
- w_up: bfloat16 [16, 4096, 768], P('ep', 'rep'), may hold values from -0.09375 to 0.09375
- w_down: bfloat16 [16, 768, 4096], P('ep', None, 'rep'), may hold values from -0.21875 to 0.21875
Outputs:
- mixed: bfloat16 [2048, 4096], P('ep', 'rep')
- grad_gate: bfloat16 [16, 4096, 768], P('ep', 'rep')
- grad_up: bfloat16 [16, 4096, 768], P('ep', 'rep')
- grad_down: bfloat16 [16, 768, 4096], P('ep', None, 'rep')
Inputs may be any that keep to these rules, and one draw needn't show every extreme that they name: `routes`: each row names 8 different experts. In each owner's block of 128 rows no expert is named by more than 80 rows, a bound that some block reaches. A token row's pairing counts from the first context row of its own block.
All inputs are finite; a program needn't handle non-finite values.
Results may differ from a plain program's by a relative error of at most 0.01.
Values may be sent and summed in bfloat16 or wider, within the bound.
A program may use at most 128 MiB of HBM per device.

v0:
```python
import jax
import jax.numpy as jnp
from jax import lax
from jax.sharding import PartitionSpec as P

D = 4096
TOP = 8


epsilon = 1e-06


def route_slots(block_routes, experts):
    flat = block_routes.reshape(-1)
    onehot = (flat[:, None] == jnp.arange(experts, dtype=jnp.int32)[None, :]).astype(jnp.int32)
    position = jnp.sum(jnp.cumsum(onehot, axis=0) * onehot, axis=1) - 1
    return (flat, position)


def swish(gate, upper):
    return gate * jax.nn.sigmoid(gate) * upper


def local(signal, routes, gates, pairing, w_gate, w_up, w_down):
    experts = lax.axis_size("ep")
    shards = lax.axis_size("rep")
    row_count = signal.shape[0]
    width = signal.shape[1]
    tokens = pairing.shape[0]
    contexts = row_count - tokens
    capacity = min(row_count, row_count * TOP * 5 // (4 * experts))
    slot_total = experts * capacity
    quarter = slot_total // shards
    route_count = row_count * TOP
    flat, position = route_slots(routes, experts)
    route_slot = flat * capacity + position
    slot_route = (
        jnp.full((slot_total,), route_count, jnp.int32)
        .at[route_slot]
        .set(jnp.arange(route_count, dtype=jnp.int32))
    )
    padded = jnp.concatenate([signal, jnp.zeros((1, width), jnp.bfloat16)], axis=0)
    outgoing = padded[slot_route // TOP].reshape(experts, capacity, width)
    arrived = lax.all_to_all(outgoing, "ep", split_axis=0, concat_axis=0, tiled=True).reshape(
        slot_total, width
    )
    gate_weight = w_gate[0]
    up_weight = w_up[0]
    down_weight = w_down[0]
    hidden_width = gate_weight.shape[1]
    gate_all, upper_all = lax.psum(
        (
            jnp.dot(arrived, gate_weight, preferred_element_type=jnp.float32),
            jnp.dot(arrived, up_weight, preferred_element_type=jnp.float32),
        ),
        "rep",
    )
    hidden_all = swish(gate_all, upper_all).astype(jnp.bfloat16)
    offset = lax.axis_index("rep") * quarter
    gate_own = lax.dynamic_slice_in_dim(gate_all, offset, quarter, 0)
    upper_own = lax.dynamic_slice_in_dim(upper_all, offset, quarter, 0)
    expert_rows = jnp.dot(hidden_all, down_weight, preferred_element_type=jnp.float32).astype(
        jnp.bfloat16
    )
    returned = lax.all_to_all(
        expert_rows.reshape(experts, capacity, width), "ep", split_axis=0, concat_axis=0, tiled=True
    ).reshape(slot_total, width)
    picked = returned[route_slot].astype(jnp.float32).reshape(row_count, TOP, width)
    combined = jnp.sum(picked * gates[:, :, None], axis=1)
    mixed = combined.astype(jnp.bfloat16)
    pair_table = (pairing[:, None] == jnp.arange(contexts, dtype=jnp.int32)[None, :]).astype(
        jnp.float32
    )
    squares_part = jnp.sum(combined * combined, axis=1)
    squares = lax.psum(squares_part, "rep")
    scale = lax.rsqrt(squares / D + epsilon)
    normed = combined * scale[:, None]
    diff = normed[:tokens] - jnp.dot(pair_table, normed[tokens:], precision=lax.Precision.HIGHEST)
    grad_normed = (
        jnp.concatenate(
            [diff, -jnp.dot(pair_table.T, diff, precision=lax.Precision.HIGHEST)], axis=0
        )
        / tokens
    )
    dots = lax.psum(jnp.sum(grad_normed * normed, axis=1), "rep")
    grad_rows = scale[:, None] * (grad_normed - normed * (dots / D)[:, None])
    route_grads = (
        (grad_rows[:, None, :] * gates[:, :, None]).astype(jnp.bfloat16).reshape(route_count, width)
    )
    padded_grads = jnp.concatenate([route_grads, jnp.zeros((1, width), jnp.bfloat16)], axis=0)
    grad_outgoing = padded_grads[slot_route].reshape(experts, capacity, width)
    grad_arrived = lax.all_to_all(
        grad_outgoing, "ep", split_axis=0, concat_axis=0, tiled=True
    ).reshape(slot_total, width)
    grad_down = lax.dot_general(
        hidden_all, grad_arrived, (((0,), (0,)), ((), ())), preferred_element_type=jnp.float32
    )
    grad_hidden = lax.psum_scatter(
        lax.dot_general(
            grad_arrived, down_weight, (((1,), (1,)), ((), ())), preferred_element_type=jnp.float32
        ),
        "rep",
        scatter_dimension=0,
        tiled=True,
    )
    sigma = jax.nn.sigmoid(gate_own)
    grad_gate_rows = (grad_hidden * upper_own * sigma * (1.0 + gate_own * (1.0 - sigma))).astype(
        jnp.bfloat16
    )
    grad_upper_rows = (grad_hidden * gate_own * sigma).astype(jnp.bfloat16)
    grad_preact = lax.all_gather(
        jnp.concatenate([grad_gate_rows, grad_upper_rows], axis=1), "rep", axis=0, tiled=True
    )
    grad_both = lax.dot_general(
        arrived, grad_preact, (((0,), (0,)), ((), ())), preferred_element_type=jnp.float32
    )
    grad_gate = grad_both[:, :hidden_width].astype(jnp.bfloat16)[None]
    grad_upper = grad_both[:, hidden_width:].astype(jnp.bfloat16)[None]
    return (mixed, grad_gate, grad_upper, grad_down.astype(jnp.bfloat16)[None])


def solution(mesh):
    return jax.shard_map(
        local,
        mesh=mesh,
        in_specs=(
            P("ep", "rep"),
            P("ep", None),
            P("ep", None),
            P("ep"),
            P("ep", "rep", None),
            P("ep", "rep", None),
            P("ep", None, "rep"),
        ),
        out_specs=(
            P("ep", "rep"),
            P("ep", "rep", None),
            P("ep", "rep", None),
            P("ep", None, "rep"),
        ),
        check_vma=False,
    )
```

profile of v0, /device:TPU:0, one launch (start us, length us, event | category | flops | bytes accessed | tf_op | source)
XLA Modules:
  0.0 800.1 jit_solution(12864587210909201167)
XLA Ops:
  9.3 4.5 reduce-window.6
  14.3 4.3 scatter_custom_fusion
  18.7 1.9 concatenate.16
  20.6 11.9 %gather_fusion = bf16[1280,2048]{1,0:T(8,128)(2,1)} fusion(bf16[129,2048]{1,0:T(8,128)(2,1)} %concatenate.16, s32[2048]{0:T(1024)S(1)} %get-tuple-element.15), kind=kCustom, calls=%fused_computation | custom fusion | bytes 10490880 | tf_op jit(solution)/shard_map/gather | solution.py:43
  32.5 122.5 %all_to_all.15 = bf16[16,80,2048]{2,1,0:T(8,128)(2,1)S(1)} all-to-all(bf16[16,80,2048]{2,1,0:T(8,128)(2,1)} %bitcast.56), channel_id=1, replica_groups=mesh['rep'=2,'ep'=16] {'ep'}, dimensions={0} | all-to-all | bytes 10485760 | tf_op jit(solution)/shard_map/all_to_all | solution.py:44
  155.1 6.1 fusion.5
  161.2 6.1 fusion.7
  167.3 188.4 %all-reduce.5.cloned.1.call-done = (f32[1280,768]{1,0:T(8,128)}, f32[1280,768]{1,0:T(8,128)}) async-done(((f32[1280,768]{1,0:T(8,128)}, f32[1280,768]{1,0:T(8,128)}), (f32[1280,768]{1,0:T(8,128)}, f32[1280,768]{1,0:T(8,128)})) %all-reduce.5.cloned.1.call-update) | async-done | bytes 7864336 | tf_op jit(solution)/shard_map/psum | solution.py:51
  355.7 4.4 multiply_convert_fusion
  360.2 6.1 convolution_convert_fusion.1
  366.3 5.8 all-to-all-start.1
  372.5 95.5 %all-to-all-done.1 = bf16[16,80,2048]{2,1,0:T(8,128)(2,1)} async-done(((bf16[16,80,2048]{2,1,0:T(8,128)(2,1)}), bf16[16,80,2048]{2,1,0:T(8,128)(2,1)}, u32[]{:S(2)}, u32[]{:S(2)}) %all-to-all-start.1) | async-done | bytes 5242912 | tf_op jit(solution)/shard_map/all_to_all | solution.py:65
  468.0 12.0 %gather_fusion.1 = bf16[1024,2048]{1,0:T(8,128)(2,1)} fusion(bf16[1280,2048]{1,0:T(8,128)(2,1)} %bitcast.10, s32[1024]{0:T(1024)S(1)} %broadcast_clamp_fusion), kind=kCustom, calls=%fused_computation.1 | custom fusion | bytes 8392704 | tf_op jit(solution)/shard_map/gather | solution.py:68
  480.0 6.5 fusion
  486.5 1.0 copy-done.3
  487.6 4.9 psum.30
  492.6 2.6 broadcast_multiply_fusion
  496.8 4.9 psum.31
  501.7 1.7 subtract_multiply_fusion
  503.4 0.9 fusion.1
  504.3 2.3 concatenate.18
  506.7 13.6 %gather_fusion.2 = bf16[1280,2048]{1,0:T(8,128)(2,1)} fusion(bf16[1025,2048]{1,0:T(8,128)(2,1)} %concatenate.18, s32[2048]{0:T(1024)S(1)} %get-tuple-element.14), kind=kCustom, calls=%fused_computation.2 | custom fusion | bytes 10490880 | tf_op jit(solution)/shard_map/gather | solution.py:91
  520.2 138.8 %all_to_all.16 = bf16[16,80,2048]{2,1,0:T(8,128)(2,1)S(1)} all-to-all(bf16[16,80,2048]{2,1,0:T(8,128)(2,1)} %bitcast.57), channel_id=1, replica_groups=mesh['rep'=2,'ep'=16] {'ep'}, dimensions={0} | all-to-all | bytes 10485760 | tf_op jit(solution)/shard_map/all_to_all | solution.py:92
  659.1 2.3 copy-done.5
  661.3 6.2 fusion.2
  667.6 51.8 %reduce-scatter.2.cloned.1.call-done = f32[640,768]{1,0:T(8,128)} async-done(((f32[1280,768]{1,0:T(8,128)}), f32[640,768]{1,0:T(8,128)}) %reduce-scatter.2.cloned.1.call-update) | async-done | bytes 1966096 | tf_op jit(solution)/shard_map/reduce_scatter | solution.py:98
  719.4 3.6 multiply_convert_fusion.2
  723.1 1.4 pad_maximum_fusion
  724.5 9.0 %fusion.9 = bf16[1,768,2048]{2,1,0:T(8,128)(2,1)} fusion(bf16[1280,768]{1,0:T(8,128)(2,1)} %copy-done.6, bf16[1280,2048]{1,0:T(8,128)(2,1)} %bitcast.62), kind=kOutput, calls=%fused_computation.21 | convolution fusion | flops 4028104704 | bytes 10354688 | tf_op jit(solution)/shard_map/dot_general | solution.py:95
  733.5 44.9 %all-gather.2.cloned.1.call-done = bf16[1280,1536]{1,0:T(8,128)(2,1)} async-done(((bf16[640,1536]{1,0:T(8,128)(2,1)}), bf16[1280,1536]{1,0:T(8,128)(2,1)}) %all-gather.2.cloned.1.call-update) | async-done | bytes 3932176 | tf_op jit(solution)/shard_map/all_gather | solution.py:111
  778.5 11.5 %convolution_convert_fusion = bf16[2048,1536]{1,0:T(8,128)(2,1)S(1)} fusion(bf16[1280,2048]{1,0:T(8,128)(2,1)} %bitcast.60, bf16[1280,1536]{1,0:T(8,128)(2,1)} %all-gather.2.cloned.1.call-done), kind=kOutput, calls=%fused_computation.8 | convolution fusion | flops 8056209408 | bytes 15466496 | tf_op jit(solution)/shard_map/dot_general | solution.py:114
  790.0 3.1 slice_bitcast_fusion
  (54 shorter events, 4.9 us)
Async XLA Ops:
  7.2 353.0 %copy-start = (bf16[1,768,2048]{2,1,0:T(8,128)(2,1)S(1)}, bf16[1,768,2048]{2,1,0:T(8,128)(2,1)}, u32[]{:S(2)}) copy-start(bf16[1,768,2048]{2,1,0:T(8,128)(2,1)} %param.13) | copy-start | bytes 9437188
  7.2 348.6 %all-reduce.5.cloned.1.call-start = ((), (), s32[]{:S(2)}) async-start(), calls=%async_computation.6 | async-start | bytes 15728640 | tf_op jit(solution)/shard_map/psum | solution.py:51
  32.5 122.5 %copy-start.9 = (bf16[1,2048,768]{2,1,0:T(8,128)(2,1)S(1)}, bf16[1,2048,768]{2,1,0:T(8,128)(2,1)}, u32[]{:S(2)}) copy-start(bf16[1,2048,768]{2,1,0:T(8,128)(2,1)} %param.12) | copy-start | bytes 9437188
  155.1 6.1 copy-start.4
  155.1 6.1 copy-start.10
  360.2 6.1 copy-start.6
  366.3 6.1 copy-start.7
  366.3 101.7 %all-to-all-start.1 = ((bf16[16,80,2048]{2,1,0:T(8,128)(2,1)}), bf16[16,80,2048]{2,1,0:T(8,128)(2,1)}, u32[]{:S(2)}, u32[]{:S(2)}) async-start(bf16[16,80,2048]{2,1,0:T(8,128)(2,1)} %bitcast.63), calls=%async_computation.1 | async-start | bytes 10485760 | tf_op jit(solution)/shard_map/all_to_all | solution.py:65
  372.1 347.4 %reduce-scatter.2.cloned.1.call-start = ((), (), s32[]{:S(2)}) async-start(), calls=%async_computation.4 | async-start | bytes 5898240 | tf_op jit(solution)/shard_map/reduce_scatter | solution.py:98
  480.0 15.2 %copy-start.8 = (s32[96]{0:T(128)S(1)}, s32[96]{0:T(128)}, u32[]{:S(2)}) copy-start(s32[96]{0:T(128)} %param.10) | copy-start | bytes 1156
  486.5 1.0 copy-start.3
  495.2 1.0 copy-start.2
  495.7 0.9 copy-start.1
  659.1 2.3 copy-start.5
  667.5 110.9 %all-gather.2.cloned.1.call-start = ((), (), s32[]{:S(2)}) async-start(), calls=%async_computation.5 | async-start | bytes 5898240 | tf_op jit(solution)/shard_map/all_gather | solution.py:111
Sparse Core Ops, SparseCore 0:
  167.5 188.2 all-reduce.4
  667.7 51.7 reduce-scatter.1
  724.6 53.8 all-gather.1
where the time goes:
time: 804 us; the launch traced here: 800 us
  waiting for transfers between devices  381 us (47%)
  blocking collectives  271 us (34%)
  local copies, waits for them, and re-layouts  54.5 us (7%)
  matrix products  46.1 us (6%)
  other arithmetic  27.1 us (3%)
  between operations  14.4 us (2%)
    psum x1, waiting for transfers between devices, local(): lax.psum((jnp.dot(arrived, gate_weight, preferred_element_type=jnp.float3...  188 us
    all_to_all x1, blocking collectives, local(): lax.all_to_all(grad_outgoing, 'ep', split_axis=0, concat_axis=0, tiled=True)  139 us
    all_to_all x1, blocking collectives, local(): lax.all_to_all(outgoing, 'ep', split_axis=0, concat_axis=0, tiled=True)  123 us
    all_to_all x1, waiting for transfers between devices, local(): lax.all_to_all(expert_rows.reshape(experts, capacity, width), 'ep', split...  95.5 us
    reduce_scatter x1, waiting for transfers between devices, local(): lax.psum_scatter(lax.dot_general(grad_arrived, down_weight, (((1,), (1,))...  51.8 us
    all_gather x1, waiting for transfers between devices, local(): lax.all_gather(jnp.concatenate([grad_gate_rows, grad_upper_rows], axis=1)...  44.9 us
  transfers between devices with their start and end apart: 4, of which 4 were waited for; matrix products, arithmetic and copies ran while one was open for 1% of the time, Pallas kernels for 0%

commit v1 on v0

v1 whole, which is shorter than its diff:
```python
import jax
import jax.numpy as jnp
from jax import lax
from jax.sharding import PartitionSpec as P

D = 4096
TOP = 8
EPSILON = 1e-06
BF = jnp.bfloat16
F32 = jnp.float32


def mm(a, b, ca=1, cb=0):
    return lax.dot_general(a, b, (((ca,), (cb,)), ((), ())), preferred_element_type=F32)


def blocks_mm(a, b, ca, cb):
    return lax.dot_general(a, b, (((ca,), (cb,)), ((0,), (0,))), preferred_element_type=F32)


def swap(value):
    return lax.ppermute(value, "rep", [(0, 1), (1, 0)])


def both_halves(own, other, rank):
    return jnp.where(
        rank == 0, jnp.concatenate([own, other], 0), jnp.concatenate([other, own], 0)
    )


def half_sum(value, rank):
    half = value.shape[0] // 2
    theirs = lax.dynamic_slice_in_dim(value, (1 - rank) * half, half, 0)
    mine = lax.dynamic_slice_in_dim(value, rank * half, half, 0)
    return mine.astype(F32) + swap(theirs).astype(F32)


def local(signal, routes, gates, pairing, w_gate, w_up, w_down):
    experts = lax.axis_size("ep")
    shards = lax.axis_size("rep")
    rank = lax.axis_index("rep")
    row_count, width = signal.shape
    tokens = pairing.shape[0]
    contexts = row_count - tokens
    capacity = min(row_count, row_count * TOP * 5 // (4 * experts))
    w_gate, w_up, w_down = w_gate[0], w_up[0], w_down[0]
    hidden_width = w_gate.shape[1]

    rows_all = lax.all_gather(signal, "ep", axis=0, tiled=True)

    expert_ids = jnp.arange(experts, dtype=jnp.int32)
    table = jnp.sum(
        jnp.where(routes[:, None, :] == expert_ids[None, :, None], gates[:, None, :], 0.0), axis=2
    )
    weight = lax.all_to_all(table.T, "ep", split_axis=0, concat_axis=0, tiled=True)
    chosen = weight > 0.0
    before = jnp.arange(row_count)[:, None] < jnp.arange(row_count)[None, :]
    position = jnp.dot(
        chosen.astype(BF), before.astype(BF), preferred_element_type=F32
    ).astype(jnp.int32)
    pick = (
        (position[:, None, :] == jnp.arange(capacity, dtype=jnp.int32)[None, :, None])
        & chosen[:, None, :]
    ).astype(BF)
    row_weight = weight.reshape(experts * row_count, 1)

    arrived = (
        blocks_mm(pick, rows_all.reshape(experts, row_count, width), 2, 1)
        .astype(BF)
        .reshape(experts * capacity, width)
    )
    gate_part = mm(arrived, w_gate)
    up_part = mm(arrived, w_up)
    if shards == 2:
        gate_own = half_sum(gate_part.astype(BF), rank)
        up_own = half_sum(up_part.astype(BF), rank)
        hidden_own = (gate_own * jax.nn.sigmoid(gate_own) * up_own).astype(BF)
        hidden = both_halves(hidden_own, swap(hidden_own), rank)
        gate_own, up_own = gate_own.astype(BF), up_own.astype(BF)
        gate_all = both_halves(gate_own, swap(gate_own), rank)
        up_all = both_halves(up_own, swap(up_own), rank)
    else:
        gate_all, up_all = lax.psum((gate_part, up_part), "rep")
        hidden = (gate_all * jax.nn.sigmoid(gate_all) * up_all).astype(BF)

    spread = (
        blocks_mm(pick, hidden.reshape(experts, capacity, hidden_width), 1, 1)
        .astype(BF)
        .reshape(experts * row_count, hidden_width)
    )
    returned = (mm(spread, w_down) * row_weight).astype(BF)
    mixed = lax.psum_scatter(returned, "ep", scatter_dimension=0, tiled=True)
    combined = mixed.astype(F32)

    pair = (pairing[:, None] == jnp.arange(contexts, dtype=jnp.int32)[None, :]).astype(F32)

    def pick_context(value):
        return jnp.dot(pair, value, precision=lax.Precision.HIGHEST)

    def per_context(value):
        return jnp.dot(pair.T, value, precision=lax.Precision.HIGHEST)

    matched = pick_context(combined[tokens:])
    sums = lax.psum(
        jnp.concatenate(
            [jnp.sum(combined * combined, axis=1), jnp.sum(combined[:tokens] * matched, axis=1)]
        ),
        "rep",
    )
    squares, cross = sums[:row_count], sums[row_count:]
    scale = lax.rsqrt(squares / D + EPSILON)
    token_scale, context_scale = scale[:tokens], scale[tokens:]
    paired_scale = jnp.sum(pair * context_scale[None, :], axis=1)
    norm_squares = squares * scale * scale
    cross = cross * token_scale * paired_scale
    paired_squares = jnp.sum(pair * norm_squares[None, tokens:], axis=1)
    dots = jnp.concatenate(
        [
            norm_squares[:tokens] - cross,
            jnp.sum(pair * (paired_squares - cross)[:, None], axis=0),
        ]
    ) / tokens
    normed = combined * scale[:, None]
    diff = normed[:tokens] - matched * paired_scale[:, None]
    grad_normed = jnp.concatenate([diff, -per_context(diff)], axis=0) / tokens
    grad_rows = (scale[:, None] * (grad_normed - normed * (dots / D)[:, None])).astype(BF)

    grads_all = lax.all_gather(grad_rows, "ep", axis=0, tiled=True)
    grad_hidden_rows = (mm(grads_all, w_down, 1, 1) * row_weight).astype(BF)
    grad_hidden_part = blocks_mm(
        pick, grad_hidden_rows.reshape(experts, row_count, hidden_width), 2, 1
    ).reshape(experts * capacity, hidden_width)
    if shards == 2:
        sent = grad_hidden_part.astype(BF)
        grad_hidden = sent.astype(F32) + swap(sent).astype(F32)
    else:
        grad_hidden = lax.psum(grad_hidden_part, "rep")
    weighted = (spread.astype(F32) * row_weight).astype(BF)
    grad_down = mm(weighted, grads_all, 0, 0).astype(BF)

    gate_all, up_all = gate_all.astype(F32), up_all.astype(F32)
    sigma = jax.nn.sigmoid(gate_all)
    grad_gate_pre = (grad_hidden * up_all * sigma * (1.0 + gate_all * (1.0 - sigma))).astype(BF)
    grad_up_pre = (grad_hidden * gate_all * sigma).astype(BF)
    grad_gate = mm(arrived, grad_gate_pre, 0, 0).astype(BF)
    grad_up = mm(arrived, grad_up_pre, 0, 0).astype(BF)
    return (mixed, grad_gate[None], grad_up[None], grad_down[None])


def solution(mesh):
    return jax.shard_map(
        local,
        mesh=mesh,
        in_specs=(
            P("ep", "rep"),
            P("ep", None),
            P("ep", None),
            P("ep"),
            P("ep", "rep", None),
            P("ep", "rep", None),
            P("ep", None, "rep"),
        ),
        out_specs=(
            P("ep", "rep"),
            P("ep", "rep", None),
            P("ep", "rep", None),
            P("ep", None, "rep"),
        ),
        check_vma=False,
    )
```

time: 804 us -> 490 us (0.61)
  blocking collectives: 271 us -> 4.94 us
  local copies, waits for them, and re-layouts: 54.5 us -> 4.58 us
  matrix products: 46.1 us -> 59.1 us
  other arithmetic: 27.1 us -> 15 us
  starting transfers between devices: 6.13 us -> 14.6 us
    all_to_all x2 -> x0, blocking collectives: 261 us -> none  [the longest x1 139 us: local(): lax.all_to_all(grad_outgoing, 'ep', split_axis=0, concat_axis=0, tiled=True)]
    psum x1 -> x0, waiting for transfers between devices: 188 us -> none  [local(): lax.psum((jnp.dot(arrived, gate_weight, preferred_element_type=jnp.float3...]
    ppermute x0 -> x6, waiting for transfers between devices: none -> 128 us  [swap(): return lax.ppermute(value, 'rep', [(0, 1), (1, 0)])]
    all_gather x1 -> x2, waiting for transfers between devices: 44.9 us -> 139 us  [the longest x1 74.8 us: local(): grads_all = lax.all_gather(grad_rows, 'ep', axis=0, tiled=True)]
    all_to_all x1, waiting for transfers between devices: 95.5 us -> 6.27 us  [local(): lax.all_to_all(table.T, 'ep', split_axis=0, concat_axis=0, tiled=True)]
    reduce_scatter x1, waiting for transfers between devices: 51.8 us -> 103 us  [local(): mixed = lax.psum_scatter(returned, 'ep', scatter_dimension=0, tiled=True)]
    gather x3 -> x0, local copies, waits for them, and re-layouts: 37.5 us -> none  [the longest x1 13.6 us: local(): grad_outgoing = padded_grads[slot_route].reshape(experts, capacity, width)]
    dot_general x8 -> x13, matrix products: 46.1 us -> 59.1 us  [the longest x7 49.6 us: mm(): lax.dot_general(a, b, (((ca,), (cb,)), ((), ())), preferred_element_type=...]
  transfers between devices with their start and end apart: 4 -> 10, of which waited for: 4 -> 9; matrix products, arithmetic and copies ran while one was open for 1% -> 4% of each run, Pallas kernels for 0% -> 0%
where the time goes in v1:
time: 490 us
  waiting for transfers between devices  377 us (77%)
  matrix products  59.1 us (12%)
  other arithmetic  15 us (3%)
  starting transfers between devices  14.6 us (3%)
  between operations  14 us (3%)
  blocking collectives  4.94 us (1%)
    ppermute x6, waiting for transfers between devices, swap(): return lax.ppermute(value, 'rep', [(0, 1), (1, 0)])  128 us
    reduce_scatter x1, waiting for transfers between devices, local(): mixed = lax.psum_scatter(returned, 'ep', scatter_dimension=0, tiled=True)  103 us
    all_gather x1, waiting for transfers between devices, local(): grads_all = lax.all_gather(grad_rows, 'ep', axis=0, tiled=True)  74.8 us
    all_gather x1, waiting for transfers between devices, local(): rows_all = lax.all_gather(signal, 'ep', axis=0, tiled=True)  64.6 us
    dot_general x7, matrix products, mm(): lax.dot_general(a, b, (((ca,), (cb,)), ((), ())), preferred_element_type=...  49.6 us
  transfers between devices with their start and end apart: 10, of which 9 were waited for; matrix products, arithmetic and copies ran while one was open for 4% of the time, Pallas kernels for 0%

profile of v1, /device:TPU:0, one launch (start us, length us, event | category | flops | bytes accessed | tf_op | source)
XLA Modules:
  0.0 489.6 jit_solution(8423610300165197743)
XLA Ops:
  7.9 1.5 select_reduce_fusion
  9.4 7.4 %all-to-all-start = ((f32[16,1,128]{2,1,0:T(1,128)}), f32[16,1,128]{2,1,0:T(1,128)S(1)}, u32[]{:S(2)}, u32[]{:S(2)}) async-start(f32[16,1,128]{2,1,0:T(1,128)} %bitcast.2), calls=%async_computation | async-start | bytes 16384 | tf_op jit(solution)/shard_map/all_to_all | solution.py:55
  16.9 6.3 %all-to-all-done = f32[16,1,128]{2,1,0:T(1,128)S(1)} async-done(((f32[16,1,128]{2,1,0:T(1,128)}), f32[16,1,128]{2,1,0:T(1,128)S(1)}, u32[]{:S(2)}, u32[]{:S(2)}) %all-to-all-start) | async-done | bytes 8224 | tf_op jit(solution)/shard_map/all_to_all | solution.py:55
  23.3 64.6 %all-gather.3.cloned.1.call-done = bf16[2048,2048]{1,0:T(8,128)(2,1)} async-done(((bf16[128,2048]{1,0:T(8,128)(2,1)}), bf16[2048,2048]{1,0:T(8,128)(2,1)}) %all-gather.3.cloned.1.call-update) | async-done | bytes 8388624 | tf_op jit(solution)/shard_map/all_gather | solution.py:49
  87.9 5.0 %convolution_convert_fusion = bf16[16,80,2048]{2,1,0:T(8,128)(2,1)S(1)} fusion(bf16[16,128,2048]{2,1,0:T(8,128)(2,1)} %bitcast.44, s32[16,128]{1,0:T(8,128)S(1)} %convolution_convert_fusion.8, pred[16,128]{1,0:T(8,128)(4,1)S(1)} %compare_bitcast_fusion), kind=kOutput, calls=%fused_computation.6 | convolution fusion | flops 674037760 | bytes 13641728 | tf_op jit(solution)/shard_map/dot_general | solution.py:18
  93.0 4.3 convolution_convert_fusion.4
  98.4 1.5 collective-permute-start.1
  99.9 4.3 convolution_convert_fusion.5
  106.3 17.0 %collective-permute-done.1 = bf16[640,768]{1,0:T(8,128)(2,1)} collective-permute-done((bf16[640,768]{1,0:T(8,128)(2,1)}, bf16[640,768]{1,0:T(8,128)(2,1)}, u32[]{:S(2)}, u32[]{:S(2)}) %collective-permute-start.1) | collective-permute-done | bytes 983072 | tf_op jit(solution)/shard_map/ppermute | solution.py:22
  123.3 20.4 %collective-permute-done = bf16[640,768]{1,0:T(8,128)(2,1)} collective-permute-done((bf16[640,768]{1,0:T(8,128)(2,1)}, bf16[640,768]{1,0:T(8,128)(2,1)}, u32[]{:S(2)}, u32[]{:S(2)}) %collective-permute-start) | collective-permute-done | bytes 983072 | tf_op jit(solution)/shard_map/ppermute | solution.py:22
  143.7 4.5 fusion.26
  148.2 1.5 collective-permute-start.2
  149.7 21.9 %collective-permute-done.2 = bf16[640,768]{1,0:T(8,128)(2,1)} collective-permute-done((bf16[640,768]{1,0:T(8,128)(2,1)}, bf16[640,768]{1,0:T(8,128)(2,1)}, u32[]{:S(2)}, u32[]{:S(2)}) %collective-permute-start.2) | collective-permute-done | bytes 983072 | tf_op jit(solution)/shard_map/ppermute | solution.py:22
  171.6 2.7 maximum_select_fusion
  175.3 1.7 copy-done.4
  177.0 9.2 %multiply_convert_fusion = bf16[2048,2048]{1,0:T(8,128)(2,1)} fusion(f32[2048]{0:T(1024)S(1)} %bitcast.59, bf16[2048,768]{1,0:T(8,128)(2,1)S(1)} %bitcast.52, bf16[1,768,2048]{2,1,0:T(8,128)(2,1)S(1)} %copy-done), kind=kOutput, calls=%fused_computation | convolution fusion | flops 6450839552 | bytes 14688256 | tf_op jit(solution)/shard_map/dot_general | solution.py:14
  186.3 103.0 %reduce-scatter.2.cloned.1.call-done = bf16[128,2048]{1,0:T(8,128)(2,1)} async-done(((bf16[2048,2048]{1,0:T(8,128)(2,1)}), bf16[128,2048]{1,0:T(8,128)(2,1)}) %reduce-scatter.2.cloned.1.call-update) | async-done | bytes 524304 | tf_op jit(solution)/shard_map/reduce_scatter | solution.py:92
  290.4 1.2 multiply_reduce_fusion
  291.6 2.2 fusion.31
  293.8 4.9 %psum.7 = f32[224]{0:T(256)S(1)} all-reduce(f32[224]{0:T(256)S(1)} %pad_maximum_fusion), channel_id=1, replica_groups=mesh['rep'=2,'ep'=16] {'rep'}, use_global_device_ids=true, to_apply=%region_4.5 | all-reduce | flops 224 | bytes 1792 | tf_op jit(solution)/shard_map/psum | solution.py:104
  299.1 1.2 broadcast_multiply_fusion
  300.3 1.3 slice_subtract_fusion
  302.1 1.2 fusion.30
  303.3 74.8 %all-gather.5.cloned.1.call-done = bf16[2048,2048]{1,0:T(8,128)(2,1)} async-done(((bf16[128,2048]{1,0:T(8,128)(2,1)}), bf16[2048,2048]{1,0:T(8,128)(2,1)}) %all-gather.5.cloned.1.call-update) | async-done | bytes 8388624 | tf_op jit(solution)/shard_map/all_gather | solution.py:128
  378.1 9.9 %multiply_convert_fusion.2 = bf16[2048,768]{1,0:T(8,128)(2,1)S(1)} fusion(bf16[2048,2048]{1,0:T(8,128)(2,1)} %all-gather.5.cloned.1.call-done, bf16[1,768,2048]{2,1,0:T(8,128)(2,1)S(1)} %copy-done, f32[2048]{0:T(1024)S(1)} %bitcast.60), kind=kOutput, calls=%fused_computation.2 | convolution fusion | flops 6445596672 | bytes 14688256 | tf_op jit(solution)/shard_map/dot_general | solution.py:14
  388.7 1.6 collective-permute-start.3
  390.8 1.5 collective-permute-start.4
  392.3 8.3 %fusion.13 = bf16[1,768,2048]{2,1,0:T(8,128)(2,1)} fusion(bf16[2048,2048]{1,0:T(8,128)(2,1)S(1)} %copy-done.11, bf16[2048,768]{1,0:T(8,128)(2,1)S(1)} %bitcast.53, f32[2048]{0:T(1024)S(1)} %bitcast.61), kind=kOutput, calls=%fused_computation.26 | convolution fusion | flops 6448742400 | bytes 14688256 | tf_op jit(solution)/shard_map/dot_general | solution.py:14
  400.7 54.8 %collective-permute-done.5 = bf16[640,768]{1,0:T(8,128)(2,1)S(1)} collective-permute-done((bf16[640,768]{1,0:T(8,128)(2,1)S(1)}, bf16[640,768]{1,0:T(8,128)(2,1)S(1)}, u32[]{:S(2)}, u32[]{:S(2)}) %collective-permute-start.5) | collective-permute-done | bytes 983072 | tf_op jit(solution)/shard_map/ppermute | solution.py:22
  455.5 6.5 %fusion.15 = bf16[1,2048,768]{2,1,0:T(8,128)(2,1)} fusion(bf16[1280,2048]{1,0:T(8,128)(2,1)S(1)} %bitcast.49, bf16[1280,768]{1,0:T(8,128)(2,1)S(1)} %collective-permute-done.3, bf16[1280,768]{1,0:T(8,128)(2,1)S(1)} %bitcast.56, bf16[640,768]{1,0:T(8,128)(2,1)S(1)} %collective-permute-done.5, bf16[640,768]{1,0:T(8,128)(2,1)S(1)} %copy-done.8, pred[]{:T(512)S(6)} %eq.50), kind=kOutput, calls=%fused_computation.28 | convolution fusion | flops 4046782464 | bytes 14286849 | tf_op jit(solution)/shard_map/dot_general | solution.py:14
  462.0 13.9 %collective-permute-done.4 = bf16[640,768]{1,0:T(8,128)(2,1)S(1)} collective-permute-done((bf16[640,768]{1,0:T(8,128)(2,1)S(1)}, bf16[640,768]{1,0:T(8,128)(2,1)S(1)}, u32[]{:S(2)}, u32[]{:S(2)}) %collective-permute-start.4) | collective-permute-done | bytes 983072 | tf_op jit(solution)/shard_map/ppermute | solution.py:22
  475.9 7.1 %fusion.14 = bf16[1,2048,768]{2,1,0:T(8,128)(2,1)} fusion(bf16[1280,2048]{1,0:T(8,128)(2,1)S(1)} %bitcast.50, bf16[1280,768]{1,0:T(8,128)(2,1)S(1)} %collective-permute-done.3, bf16[1280,768]{1,0:T(8,128)(2,1)S(1)} %bitcast.57, bf16[640,768]{1,0:T(8,128)(2,1)S(1)} %collective-permute-done.4, bf16[640,768]{1,0:T(8,128)(2,1)S(1)} %copy-done.9, pred[]{:T(512)S(6)} %eq.50, ...), kind=kOutput, calls=%fused_computation.27 | convolution fusion | flops 4060545024 | bytes 16252929 | tf_op jit(solution)/shard_map/dot_general | solution.py:14
  (58 shorter events, 8.5 us)
Async XLA Ops:
  7.2 169.8 %copy-start = (bf16[1,768,2048]{2,1,0:T(8,128)(2,1)S(1)}, bf16[1,768,2048]{2,1,0:T(8,128)(2,1)}, u32[]{:S(2)}) copy-start(bf16[1,768,2048]{2,1,0:T(8,128)(2,1)} %param.13) | copy-start | bytes 9437188
  7.2 80.7 %all-gather.3.cloned.1.call-start = ((), (), s32[]{:S(2)}) async-start(), calls=%async_computation.2 | async-start | bytes 8912896 | tf_op jit(solution)/shard_map/all_gather | solution.py:49
  9.4 13.7 %all-to-all-start = ((f32[16,1,128]{2,1,0:T(1,128)}), f32[16,1,128]{2,1,0:T(1,128)S(1)}, u32[]{:S(2)}, u32[]{:S(2)}) async-start(f32[16,1,128]{2,1,0:T(1,128)} %bitcast.2), calls=%async_computation | async-start | bytes 16384 | tf_op jit(solution)/shard_map/all_to_all | solution.py:55
  16.8 272.4 %reduce-scatter.2.cloned.1.call-start = ((), (), s32[]{:S(2)}) async-start(), calls=%async_computation.3 | async-start | bytes 8912896 | tf_op jit(solution)/shard_map/reduce_scatter | solution.py:92
  87.9 5.1 %copy-start.12 = (bf16[1,2048,768]{2,1,0:T(8,128)(2,1)S(1)}, bf16[1,2048,768]{2,1,0:T(8,128)(2,1)}, u32[]{:S(2)}) copy-start(bf16[1,2048,768]{2,1,0:T(8,128)(2,1)} %param.12) | copy-start | bytes 9437188
  93.0 6.9 %copy-start.2 = (bf16[16,80,2048]{2,1,0:T(8,128)(2,1)}, bf16[16,80,2048]{2,1,0:T(8,128)(2,1)S(1)}, u32[]{:S(2)}) copy-start(bf16[16,80,2048]{2,1,0:T(8,128)(2,1)S(1)} %convolution_convert_fusion) | copy-start | bytes 15728644
  93.0 6.9 %copy-start.13 = (bf16[1,2048,768]{2,1,0:T(8,128)(2,1)S(1)}, bf16[1,2048,768]{2,1,0:T(8,128)(2,1)}, u32[]{:S(2)}) copy-start(bf16[1,2048,768]{2,1,0:T(8,128)(2,1)} %param.11) | copy-start | bytes 9437188
  97.3 6.9 %copy-start.6 = (bf16[1280,768]{1,0:T(8,128)(2,1)}, bf16[1280,768]{1,0:T(8,128)(2,1)S(1)}, u32[]{:S(2)}) copy-start(bf16[1280,768]{1,0:T(8,128)(2,1)S(1)} %convolution_convert_fusion.4) | copy-start | bytes 5898244
  98.4 24.9 %collective-permute-start.1 = (bf16[640,768]{1,0:T(8,128)(2,1)}, bf16[640,768]{1,0:T(8,128)(2,1)}, u32[]{:S(2)}, u32[]{:S(2)}) collective-permute-start(bf16[640,768]{1,0:T(8,128)(2,1)} %constant_dynamic-slice_fusion), channel_id=1, source_target_pairs={{0,16},{16,0},{1,17},{17,1},{2,18},{18,2},{3,19},{19,3},{4,20},{20... | collective-permute-start | bytes 2949128 | tf_op jit(solution)/shard_map/ppermute | solution.py:22
  104.2 1.6 copy-start.7
  105.8 37.9 %collective-permute-start = (bf16[640,768]{1,0:T(8,128)(2,1)}, bf16[640,768]{1,0:T(8,128)(2,1)}, u32[]{:S(2)}, u32[]{:S(2)}) collective-permute-start(bf16[640,768]{1,0:T(8,128)(2,1)} %constant_dynamic-slice_fusion.1), channel_id=1, source_target_pairs={{0,16},{16,0},{1,17},{17,1},{2,18},{18,2},{3,19},{19,3},{4,20},{20... | collective-permute-start | bytes 2949128 | tf_op jit(solution)/shard_map/ppermute | solution.py:22
  148.2 23.4 %collective-permute-start.2 = (bf16[640,768]{1,0:T(8,128)(2,1)}, bf16[640,768]{1,0:T(8,128)(2,1)}, u32[]{:S(2)}, u32[]{:S(2)}) collective-permute-start(bf16[640,768]{1,0:T(8,128)(2,1)} %get-tuple-element.9), channel_id=1, source_target_pairs={{0,16},{16,0},{1,17},{17,1},{2,18},{18,2},{3,19},{19,3},{4,20},{20... | collective-permute-start | bytes 2949128 | tf_op jit(solution)/shard_map/ppermute | solution.py:22
  175.3 1.7 copy-start.4
  186.2 105.4 %copy-start.10 = (s32[96]{0:T(128)S(1)}, s32[96]{0:T(128)}, u32[]{:S(2)}) copy-start(s32[96]{0:T(128)} %param.10) | copy-start | bytes 1156
  186.2 191.9 %all-gather.5.cloned.1.call-start = ((), (), s32[]{:S(2)}) async-start(), calls=%async_computation.4 | async-start | bytes 8912896 | tf_op jit(solution)/shard_map/all_gather | solution.py:128
  298.7 3.3 copy-start.3
  378.1 14.3 %copy-start.11 = (bf16[2048,2048]{1,0:T(8,128)(2,1)S(1)}, bf16[2048,2048]{1,0:T(8,128)(2,1)}, u32[]{:S(2)}) copy-start(bf16[2048,2048]{1,0:T(8,128)(2,1)} %all-gather.5.cloned.1.call-done) | copy-start | bytes 25165828
  388.0 2.3 copy-start.8
  388.0 2.8 copy-start.9
  388.1 4.3 copy-start.5
  388.7 66.8 %collective-permute-start.3 = (bf16[1280,768]{1,0:T(8,128)(2,1)S(1)}, bf16[1280,768]{1,0:T(8,128)(2,1)S(1)}, u32[]{:S(2)}, u32[]{:S(2)}) collective-permute-start(bf16[1280,768]{1,0:T(8,128)(2,1)S(1)} %bitcast.55), channel_id=1, source_target_pairs={{0,16},{16,0},{1,17},{17,1},{2,18},{18,2},{3,19},{19,3},{4,20},{20... | collective-permute-start | bytes 5898248 | tf_op jit(solution)/shard_map/ppermute | solution.py:22
  390.3 65.2 %collective-permute-start.5 = (bf16[640,768]{1,0:T(8,128)(2,1)S(1)}, bf16[640,768]{1,0:T(8,128)(2,1)S(1)}, u32[]{:S(2)}, u32[]{:S(2)}) collective-permute-start(bf16[640,768]{1,0:T(8,128)(2,1)S(1)} %copy-done.8), channel_id=1, source_target_pairs={{0,16},{16,0},{1,17},{17,1},{2,18},{18,2},{3,19},{19,3},{4,20},{20... | collective-permute-start | bytes 2949128 | tf_op jit(solution)/shard_map/ppermute | solution.py:22
  390.8 64.7 %slice-start = ((s8[5242880]{0:T(1024)(128)(4,1)}), s8[4194304]{0:T(1024)(128)(4,1)S(1)}, s32[]{:S(2)}) async-start(s8[5242880]{0:T(1024)(128)(4,1)} %bitcast.47), calls=%async_computation.5 | async-start | bytes 8388608
  390.8 64.7 %slice-start.1 = ((s8[5242880]{0:T(1024)(128)(4,1)}), s8[1048576]{0:T(1024)(128)(4,1)S(1)}, s32[]{:S(2)}) async-start(s8[5242880]{0:T(1024)(128)(4,1)} %bitcast.47), calls=%async_computation.6 | async-start | bytes 2097152
  390.8 85.1 %collective-permute-start.4 = (bf16[640,768]{1,0:T(8,128)(2,1)S(1)}, bf16[640,768]{1,0:T(8,128)(2,1)S(1)}, u32[]{:S(2)}, u32[]{:S(2)}) collective-permute-start(bf16[640,768]{1,0:T(8,128)(2,1)S(1)} %copy-done.9), channel_id=1, source_target_pairs={{0,16},{16,0},{1,17},{17,1},{2,18},{18,2},{3,19},{19,3},{4,20},{20... | collective-permute-start | bytes 2949128 | tf_op jit(solution)/shard_map/ppermute | solution.py:22
  475.9 7.2 %copy-start.1 = (bf16[1,768,2048]{2,1,0:T(8,128)(2,1)S(1)}, bf16[1,768,2048]{2,1,0:T(8,128)(2,1)}, u32[]{:S(2)}) copy-start(bf16[1,768,2048]{2,1,0:T(8,128)(2,1)} %param.13) | copy-start | bytes 9437188
Sparse Core Ops, SparseCore 0:
  10.2 77.6 all-gather.2
  186.3 102.8 reduce-scatter.1
  303.4 74.6 all-gather.4

commit v2 on v1

v2 whole, which is shorter than its diff:
```python
import jax
import jax.numpy as jnp
from jax import lax
from jax.sharding import PartitionSpec as P

D = 4096
TOP = 8
EPSILON = 1e-06
BF = jnp.bfloat16
F32 = jnp.float32


def mm(a, b, ca=1, cb=0):
    return lax.dot_general(a, b, (((ca,), (cb,)), ((), ())), preferred_element_type=F32)


def blocks_mm(a, b, ca, cb):
    return lax.dot_general(a, b, (((ca,), (cb,)), ((0,), (0,))), preferred_element_type=F32)


def swap(value):
    return lax.ppermute(value, "rep", [(0, 1), (1, 0)])


def both_halves(own, other, rank):
    return jnp.where(
        rank == 0, jnp.concatenate([own, other], 0), jnp.concatenate([other, own], 0)
    )


def half_sum(value, rank):
    half = value.shape[0] // 2
    theirs = lax.dynamic_slice_in_dim(value, (1 - rank) * half, half, 0)
    mine = lax.dynamic_slice_in_dim(value, rank * half, half, 0)
    return mine.astype(F32) + swap(theirs).astype(F32)


def row_gradient(combined, pairing):
    row_count, tokens = combined.shape[0], pairing.shape[0]
    contexts = row_count - tokens
    pair = (pairing[:, None] == jnp.arange(contexts, dtype=jnp.int32)[None, :]).astype(F32)

    def pick_context(value):
        return jnp.dot(pair, value, precision=lax.Precision.HIGHEST)

    def per_context(value):
        return jnp.dot(pair.T, value, precision=lax.Precision.HIGHEST)

    matched = pick_context(combined[tokens:])
    sums = lax.psum(
        jnp.concatenate(
            [jnp.sum(combined * combined, axis=1), jnp.sum(combined[:tokens] * matched, axis=1)]
        ),
        "rep",
    )
    squares, cross = sums[:row_count], sums[row_count:]
    scale = lax.rsqrt(squares / D + EPSILON)
    token_scale, context_scale = scale[:tokens], scale[tokens:]
    paired_scale = jnp.sum(pair * context_scale[None, :], axis=1)
    norm_squares = squares * scale * scale
    cross = cross * token_scale * paired_scale
    paired_squares = jnp.sum(pair * norm_squares[None, tokens:], axis=1)
    dots = jnp.concatenate(
        [
            norm_squares[:tokens] - cross,
            jnp.sum(pair * (paired_squares - cross)[:, None], axis=0),
        ]
    ) / tokens
    normed = combined * scale[:, None]
    diff = normed[:tokens] - matched * paired_scale[:, None]
    grad_normed = jnp.concatenate([diff, -per_context(diff)], axis=0) / tokens
    grad_rows = (scale[:, None] * (grad_normed - normed * (dots / D)[:, None])).astype(BF)
    return grad_rows


def gate_table(routes, gates, experts):
    expert_ids = jnp.arange(experts, dtype=jnp.int32)
    table = jnp.sum(
        jnp.where(routes[:, None, :] == expert_ids[None, :, None], gates[:, None, :], 0.0), axis=2
    )
    return lax.all_to_all(table.T, "ep", split_axis=0, concat_axis=0, tiled=True)


def slot_picks(weight, capacity):
    row_count = weight.shape[1]
    chosen = weight > 0.0
    before = jnp.arange(row_count)[:, None] < jnp.arange(row_count)[None, :]
    position = jnp.dot(
        chosen.astype(BF), before.astype(BF), preferred_element_type=F32
    ).astype(jnp.int32)
    return (
        (position[:, None, :] == jnp.arange(capacity, dtype=jnp.int32)[None, :, None])
        & chosen[:, None, :]
    ).astype(BF)


def local_general(signal, routes, gates, pairing, w_gate, w_up, w_down):
    experts = lax.axis_size("ep")
    row_count, width = signal.shape
    capacity = min(row_count, row_count * TOP * 5 // (4 * experts))
    w_gate, w_up, w_down = w_gate[0], w_up[0], w_down[0]
    hidden_width = w_gate.shape[1]

    rows_all = lax.all_gather(signal, "ep", axis=0, tiled=True)

    weight = gate_table(routes, gates, experts)
    pick = slot_picks(weight, capacity)
    row_weight = weight.reshape(experts * row_count, 1)

    arrived = (
        blocks_mm(pick, rows_all.reshape(experts, row_count, width), 2, 1)
        .astype(BF)
        .reshape(experts * capacity, width)
    )
    gate_part = mm(arrived, w_gate)
    up_part = mm(arrived, w_up)
    gate_all, up_all = lax.psum((gate_part, up_part), "rep")
    hidden = (gate_all * jax.nn.sigmoid(gate_all) * up_all).astype(BF)

    spread = (
        blocks_mm(pick, hidden.reshape(experts, capacity, hidden_width), 1, 1)
        .astype(BF)
        .reshape(experts * row_count, hidden_width)
    )
    returned = (mm(spread, w_down) * row_weight).astype(BF)
    mixed = lax.psum_scatter(returned, "ep", scatter_dimension=0, tiled=True)
    combined = mixed.astype(F32)

    grad_rows = row_gradient(combined, pairing)
    grads_all = lax.all_gather(grad_rows, "ep", axis=0, tiled=True)
    grad_hidden_rows = (mm(grads_all, w_down, 1, 1) * row_weight).astype(BF)
    grad_hidden_part = blocks_mm(
        pick, grad_hidden_rows.reshape(experts, row_count, hidden_width), 2, 1
    ).reshape(experts * capacity, hidden_width)
    grad_hidden = lax.psum(grad_hidden_part, "rep")
    weighted = (spread.astype(F32) * row_weight).astype(BF)
    grad_down = mm(weighted, grads_all, 0, 0).astype(BF)

    gate_all, up_all = gate_all.astype(F32), up_all.astype(F32)
    sigma = jax.nn.sigmoid(gate_all)
    grad_gate_pre = (grad_hidden * up_all * sigma * (1.0 + gate_all * (1.0 - sigma))).astype(BF)
    grad_up_pre = (grad_hidden * gate_all * sigma).astype(BF)
    grad_gate = mm(arrived, grad_gate_pre, 0, 0).astype(BF)
    grad_up = mm(arrived, grad_up_pre, 0, 0).astype(BF)
    return (mixed, grad_gate[None], grad_up[None], grad_down[None])


Z = 4


def across(value, bit):
    return lax.ppermute(value, "ep", [(i, i ^ bit) for i in range(4 * Z)])


def across_x(value, low, high):
    return lax.ppermute(
        value, "ep", [(z * 4 + i, z * 4 + (i ^ 2)) for z in range(low, high) for i in range(4)]
    )


def along_z(value, low, high, step):
    return lax.ppermute(
        value,
        "ep",
        [(z * 4 + i, (z + step) * 4 + i) for z in range(low, high) for i in range(4)],
    )


def gather_groups(value):
    up1 = along_z(value, 0, 3, 1)
    down1 = along_z(value, 1, 4, -1)
    side0 = across_x(value, 0, 4)
    up2 = along_z(up1, 1, 3, 1)
    down2 = along_z(down1, 1, 3, -1)
    side_up1 = across_x(up1, 1, 4)
    side_down1 = across_x(down1, 0, 3)
    up3 = along_z(up2, 2, 3, 1)
    down3 = along_z(down2, 1, 2, -1)
    side_up2 = across_x(up2, 2, 4)
    side_down2 = across_x(down2, 0, 2)
    side_up3 = across_x(up3, 3, 4)
    side_down3 = across_x(down3, 0, 1)
    pairs = [
        (value, side0),
        (up1 + down3, side_up1 + side_down3),
        (up2 + down2, side_up2 + side_down2),
        (up3 + down1, side_up3 + side_down1),
    ]
    groups = []
    for own, side in pairs:
        mine = jnp.concatenate([own, side], 0)
        other = across(mine, 1)
        groups.append(jnp.concatenate([mine, other], 0))
    return groups


def scatter_sum(value):
    def add(a, b):
        return (a.astype(F32) + b.astype(F32)).astype(BF)

    value = add(value[:, 0], across(value[:, 1], 1))
    value = add(value[:, 0], across(value[:, 1], 2))
    up = along_z(value[1], 0, 1, 1)
    down = along_z(value[3], 3, 4, -1)
    up = along_z(add(value[2], up), 0, 2, 1)
    down = along_z(add(value[2], down), 2, 4, -1)
    up = along_z(add(value[3], up), 0, 3, 1)
    down = along_z(add(value[1], down), 1, 4, -1)
    return value[0].astype(F32) + up.astype(F32) + down.astype(F32)


ORDER = (0, 2, 1, 3)
CHUNKS = 4


def local(signal, routes, gates, pairing, w_gate, w_up, w_down):
    experts = lax.axis_size("ep")
    rank = lax.axis_index("rep")
    me = lax.axis_index("ep")
    row_count, width = signal.shape
    capacity = min(row_count, row_count * TOP * 5 // (4 * experts))
    w_gate, w_up, w_down = w_gate[0], w_up[0], w_down[0]
    hidden_width = w_gate.shape[1]
    w_both = jnp.concatenate([w_gate, w_up], 1)

    row_groups = gather_groups(signal)
    weight = gate_table(routes, gates, experts)
    place = jnp.arange(experts, dtype=jnp.int32)
    owner = ((me // 4 - place // 4 + Z) % Z) * 4 + (me % 4) ^ (place % 2 * 2 + place // 2 % 2)
    weight = jnp.take(weight, owner, axis=0)
    pick = slot_picks(weight, capacity).reshape(Z, 4, capacity, row_count)
    row_weight = weight.reshape(Z, 4 * row_count, 1)

    arrived, hidden, gate_up, spread = [None] * Z, [None] * Z, [None] * Z, [None] * Z
    for k in ORDER:
        rows = row_groups[k].reshape(4, row_count, width)
        arrived[k] = blocks_mm(pick[k], rows, 2, 1).astype(BF).reshape(4 * capacity, width)
        own = half_sum(mm(arrived[k], w_both).astype(BF), rank)
        gate, up = own[:, :hidden_width], own[:, hidden_width:]
        hidden_own = (gate * jax.nn.sigmoid(gate) * up).astype(BF)
        gate_up[k] = own.astype(BF)
        hidden[k] = both_halves(hidden_own, swap(hidden_own), rank)
        spread[k] = (
            blocks_mm(pick[k], hidden[k].reshape(4, capacity, hidden_width), 1, 1)
            .astype(BF)
            .reshape(4 * row_count, hidden_width)
        )
    spread = jnp.concatenate(spread, 0)
    all_weight = weight.reshape(experts * row_count, 1)

    part = width // CHUNKS
    combined = []
    for c in range(CHUNKS):
        returned = (mm(spread, w_down[:, c * part : (c + 1) * part]) * all_weight).astype(BF)
        combined.append(scatter_sum(returned.reshape(Z, 2, 2, row_count, part)))
    combined = jnp.concatenate(combined, 1)
    others = [swap(value) for value in gate_up]
    combined, others = lax.optimization_barrier((combined, others))
    mixed = combined.astype(BF)
    grad_rows = row_gradient(combined, pairing)

    grad_groups = gather_groups(grad_rows)
    gate_pre, up_pre = [None] * Z, [None] * Z
    for k in ORDER:
        rows = (mm(grad_groups[k], w_down, 1, 1) * row_weight[k]).astype(BF)
        sent = (
            blocks_mm(pick[k], rows.reshape(4, row_count, hidden_width), 2, 1)
            .reshape(4 * capacity, hidden_width)
            .astype(BF)
        )
        grad_hidden = sent.astype(F32) + swap(sent).astype(F32)
        both = both_halves(gate_up[k], others[k], rank).astype(F32)
        gate, up = both[:, :hidden_width], both[:, hidden_width:]
        sigma = jax.nn.sigmoid(gate)
        gate_pre[k] = (grad_hidden * up * sigma * (1.0 + gate * (1.0 - sigma))).astype(BF)
        up_pre[k] = (grad_hidden * gate * sigma).astype(BF)
    weighted = (spread.astype(F32) * all_weight).astype(BF)
    grad_down = mm(weighted, jnp.concatenate(grad_groups, 0), 0, 0).astype(BF)
    arrived = jnp.concatenate(arrived, 0)
    grad_gate = mm(arrived, jnp.concatenate(gate_pre, 0), 0, 0).astype(BF)
    grad_up = mm(arrived, jnp.concatenate(up_pre, 0), 0, 0).astype(BF)
    return (mixed, grad_gate[None], grad_up[None], grad_down[None])


def solution(mesh):
    blocked = mesh.shape["ep"] == 4 * Z and mesh.shape["rep"] == 2
    return jax.shard_map(
        local if blocked else local_general,
        mesh=mesh,
        in_specs=(
            P("ep", "rep"),
            P("ep", None),
            P("ep", None),
            P("ep"),
            P("ep", "rep", None),
            P("ep", "rep", None),
            P("ep", None, "rep"),
        ),
        out_specs=(
            P("ep", "rep"),
            P("ep", "rep", None),
            P("ep", "rep", None),
            P("ep", None, "rep"),
        ),
        check_vma=False,
    )
```

time: 490 us -> 472 us (0.963); the launches traced: 490 us -> 466 us
  waiting for transfers between devices: 377 us -> 223 us
  starting transfers between devices: 14.6 us -> 136 us
  between operations: 14 us -> 3.13 us
  matrix products: 59.1 us -> 68.9 us
  other arithmetic: 15 us -> 23.3 us
    all_gather x2 -> x0, waiting for transfers between devices: 139 us -> none  [the longest x1 74.8 us: local(): grads_all = lax.all_gather(grad_rows, 'ep', axis=0, tiled=True)]
    ppermute x0 -> x66, waiting for transfers between devices: none -> 125 us  [the longest x36 52.1 us: along_z(): lax.ppermute(value, 'ep', [(z * 4 + i, (z + step) * 4 + i) for z in range...]
    ppermute x0 -> x66, starting transfers between devices: none -> 115 us  [the longest x36 82.8 us: along_z(): lax.ppermute(value, 'ep', [(z * 4 + i, (z + step) * 4 + i) for z in range...]
    reduce_scatter x1 -> x0, waiting for transfers between devices: 103 us -> none  [local(): mixed = lax.psum_scatter(returned, 'ep', scatter_dimension=0, tiled=True)]
    ppermute x6 -> x16, waiting for transfers between devices: 128 us -> 94.8 us  [swap(): return lax.ppermute(value, 'rep', [(0, 1), (1, 0)])]
    dot_general x7 -> x15, matrix products: 49.6 us -> 62.9 us  [mm(): lax.dot_general(a, b, (((ca,), (cb,)), ((), ())), preferred_element_type=...]
    ppermute x6 -> x16, starting transfers between devices: 7.09 us -> 14.7 us  [swap(): return lax.ppermute(value, 'rep', [(0, 1), (1, 0)])]
    add x0 -> x10, other arithmetic: none -> 5.7 us  [the longest x1 1.33 us: gather_groups(): up2 + down2]
  transfers between devices with their start and end apart: 10 -> 83, of which waited for: 9 -> 31; matrix products, arithmetic and copies ran while one was open for 4% -> 16% of each run, Pallas kernels for 0% -> 0%
where the time goes in v2:
time: 472 us; the launch traced here: 466 us
  waiting for transfers between devices  223 us (47%)
  starting transfers between devices  136 us (29%)
  matrix products  68.9 us (15%)
  other arithmetic  23.3 us (5%)
  local copies, waits for them, and re-layouts  6.16 us (1%)
  blocking collectives  4.94 us (1%)
    ppermute x16, waiting for transfers between devices, swap(): return lax.ppermute(value, 'rep', [(0, 1), (1, 0)])  94.8 us
    ppermute x36, starting transfers between devices, along_z(): lax.ppermute(value, 'ep', [(z * 4 + i, (z + step) * 4 + i) for z in range...  82.8 us
    dot_general x15, matrix products, mm(): lax.dot_general(a, b, (((ca,), (cb,)), ((), ())), preferred_element_type=...  62.9 us
    ppermute x36, waiting for transfers between devices, along_z(): lax.ppermute(value, 'ep', [(z * 4 + i, (z + step) * 4 + i) for z in range...  52.1 us
    ppermute x14, waiting for transfers between devices, across_x(): lax.ppermute(value, 'ep', [(z * 4 + i, z * 4 + (i ^ 2)) for z in range(lo...  37.4 us
    ppermute x16, waiting for transfers between devices, across(): return lax.ppermute(value, 'ep', [(i, i ^ bit) for i in range(4 * Z)])  35.8 us
    ppermute x14, starting transfers between devices, across_x(): lax.ppermute(value, 'ep', [(z * 4 + i, z * 4 + (i ^ 2)) for z in range(lo...  26.1 us
    ppermute x16, starting transfers between devices, swap(): return lax.ppermute(value, 'rep', [(0, 1), (1, 0)])  14.7 us
  transfers between devices with their start and end apart: 83, of which 31 were waited for; matrix products, arithmetic and copies ran while one was open for 16% of the time, Pallas kernels for 0%

profile of v2, /device:TPU:0, one launch (start us, length us, event | category | flops | bytes accessed | tf_op | source)
XLA Modules:
  0.0 465.8 jit_solution(11517844394859365612)
XLA Ops:
  9.2 6.6 %collective-permute-done = bf16[128,2048]{1,0:T(8,128)(2,1)S(1)} collective-permute-done((bf16[128,2048]{1,0:T(8,128)(2,1)}, bf16[128,2048]{1,0:T(8,128)(2,1)S(1)}, u32[]{:S(2)}, u32[]{:S(2)}) %collective-permute-start) | collective-permute-done | bytes 524320 | tf_op jit(solution)/shard_map/ppermute | solution.py:156
  18.3 6.3 %all-to-all-start = ((f32[16,1,128]{2,1,0:T(1,128)}), f32[16,1,128]{2,1,0:T(1,128)S(1)}, u32[]{:S(2)}, u32[]{:S(2)}) async-start(f32[16,1,128]{2,1,0:T(1,128)} %bitcast.2), calls=%async_computation | async-start | bytes 16384 | tf_op jit(solution)/shard_map/all_to_all | solution.py:81
  32.4 12.3 %collective-permute-done.6 = bf16[128,2048]{1,0:T(8,128)(2,1)} collective-permute-done((bf16[128,2048]{1,0:T(8,128)(2,1)S(1)}, bf16[128,2048]{1,0:T(8,128)(2,1)}, u32[]{:S(2)}, u32[]{:S(2)}) %collective-permute-start.6) | collective-permute-done | bytes 524320 | tf_op jit(solution)/shard_map/ppermute | solution.py:162
  89.1 10.5 %collective-permute-done.17 = bf16[160,1536]{1,0:T(8,128)(2,1)S(1)} collective-permute-done((bf16[160,1536]{1,0:T(8,128)(2,1)S(1)}, bf16[160,1536]{1,0:T(8,128)(2,1)S(1)}, u32[]{:S(2)}, u32[]{:S(2)}) %collective-permute-start.17) | collective-permute-done | bytes 491552 | tf_op jit(solution)/shard_map/ppermute | solution.py:22
  111.1 30.6 %collective-permute-done.23 = bf16[160,1536]{1,0:T(8,128)(2,1)S(1)} collective-permute-done((bf16[160,1536]{1,0:T(8,128)(2,1)S(1)}, bf16[160,1536]{1,0:T(8,128)(2,1)S(1)}, u32[]{:S(2)}, u32[]{:S(2)}) %collective-permute-start.23) | collective-permute-done | bytes 491552 | tf_op jit(solution)/shard_map/ppermute | solution.py:22
  143.0 11.7 %collective-permute-done.11 = bf16[160,1536]{1,0:T(8,128)(2,1)S(1)} collective-permute-done((bf16[160,1536]{1,0:T(8,128)(2,1)S(1)}, bf16[160,1536]{1,0:T(8,128)(2,1)S(1)}, u32[]{:S(2)}, u32[]{:S(2)}) %collective-permute-start.11) | collective-permute-done | bytes 491552 | tf_op jit(solution)/shard_map/ppermute | solution.py:22
  157.1 6.5 %collective-permute-done.24 = bf16[160,768]{1,0:T(8,128)(2,1)S(1)} collective-permute-done((bf16[160,768]{1,0:T(8,128)(2,1)S(1)}, bf16[160,768]{1,0:T(8,128)(2,1)S(1)}, u32[]{:S(2)}, u32[]{:S(2)}) %collective-permute-start.24) | collective-permute-done | bytes 245792 | tf_op jit(solution)/shard_map/ppermute | solution.py:22
  168.2 5.6 %multiply_convert_fusion.1 = bf16[2048,512]{1,0:T(8,128)(2,1)S(1)} fusion(f32[2048]{0:T(1024)S(1)} %bitcast.250, bf16[768,2048]{1,0:T(8,128)(2,1)S(1)} %bitcast.263, bf16[512,768]{1,0:T(8,128)(2,1)S(1)} %bitcast.279, bf16[512,768]{1,0:T(8,128)(2,1)S(1)} %bitcast.284, bf16[512,768]{1,0:T(8,128)(2,1)S(1)} %bitcast.289, bf16[512,768]{1,0:T(8,128)(2,1)S(1)} %bitcast.294), kind=kOutput, calls=%fused_computation.4 | convolution fusion | flops 1625292800 | bytes 6037504 | tf_op jit(solution)/shard_map/dot_general | solution.py:14
  173.8 5.2 %multiply_convert_fusion.2 = bf16[2048,512]{1,0:T(8,128)(2,1)S(1)} fusion(f32[2048]{0:T(1024)S(1)} %bitcast.251, bf16[768,2048]{1,0:T(8,128)(2,1)S(1)} %bitcast.264, bf16[512,768]{1,0:T(8,128)(2,1)S(1)} %bitcast.280, bf16[512,768]{1,0:T(8,128)(2,1)S(1)} %bitcast.285, bf16[512,768]{1,0:T(8,128)(2,1)S(1)} %bitcast.290, bf16[512,768]{1,0:T(8,128)(2,1)S(1)} %bitcast.295), kind=kOutput, calls=%fused_computation.5 | convolution fusion | flops 1625292800 | bytes 6037504 | tf_op jit(solution)/shard_map/dot_general | solution.py:14
  179.0 5.2 %multiply_convert_fusion.3 = bf16[2048,512]{1,0:T(8,128)(2,1)S(1)} fusion(f32[2048]{0:T(1024)S(1)} %bitcast.252, bf16[768,2048]{1,0:T(8,128)(2,1)S(1)} %bitcast.265, bf16[512,768]{1,0:T(8,128)(2,1)S(1)} %bitcast.281, bf16[512,768]{1,0:T(8,128)(2,1)S(1)} %bitcast.286, bf16[512,768]{1,0:T(8,128)(2,1)S(1)} %bitcast.291, bf16[512,768]{1,0:T(8,128)(2,1)S(1)} %bitcast.296), kind=kOutput, calls=%fused_computation.6 | convolution fusion | flops 1625292800 | bytes 6037504 | tf_op jit(solution)/shard_map/dot_general | solution.py:14
  185.4 5.4 %multiply_convert_fusion.4 = bf16[2048,512]{1,0:T(8,128)(2,1)S(1)} fusion(f32[2048]{0:T(1024)S(1)} %bitcast.253, bf16[768,2048]{1,0:T(8,128)(2,1)S(1)} %bitcast.266, bf16[512,768]{1,0:T(8,128)(2,1)S(1)} %bitcast.282, bf16[512,768]{1,0:T(8,128)(2,1)S(1)} %bitcast.287, bf16[512,768]{1,0:T(8,128)(2,1)S(1)} %bitcast.292, bf16[512,768]{1,0:T(8,128)(2,1)S(1)} %bitcast.297), kind=kOutput, calls=%fused_computation.7 | convolution fusion | flops 1625292800 | bytes 6037504 | tf_op jit(solution)/shard_map/dot_general | solution.py:14
  196.6 10.4 %collective-permute-done.50 = bf16[4,128,512]{2,1,0:T(8,128)(2,1)S(1)} collective-permute-done((bf16[4,128,512]{2,1,0:T(8,128)(2,1)S(1)}, bf16[4,128,512]{2,1,0:T(8,128)(2,1)S(1)}, u32[]{:S(2)}, u32[]{:S(2)}) %collective-permute-start.50) | collective-permute-done | bytes 524320 | tf_op jit(solution)/shard_map/ppermute | solution.py:152
  208.3 10.0 %collective-permute-done.42 = bf16[4,128,512]{2,1,0:T(8,128)(2,1)S(1)} collective-permute-done((bf16[4,128,512]{2,1,0:T(8,128)(2,1)S(1)}, bf16[4,128,512]{2,1,0:T(8,128)(2,1)S(1)}, u32[]{:S(2)}, u32[]{:S(2)}) %collective-permute-start.42) | collective-permute-done | bytes 524320 | tf_op jit(solution)/shard_map/ppermute | solution.py:152
  218.3 5.3 %collective-permute-start.51 = (bf16[128,512]{1,0:T(8,128)(2,1)S(1)}, bf16[128,512]{1,0:T(8,128)(2,1)S(1)}, u32[]{:S(2)}, u32[]{:S(2)}) collective-permute-start(bf16[128,512]{1,0:T(8,128)(2,1)S(1)} %get-tuple-element.82), channel_id=1, source_target_pairs={{0,4},{1,5},{2,6},{3,7},{16,20},{17,21},{18,22},{19,23}} | collective-permute-start | bytes 393224 | tf_op jit(solution)/shard_map/ppermute | solution.py:162
  223.8 5.7 %collective-permute-done.34 = bf16[4,128,512]{2,1,0:T(8,128)(2,1)S(1)} collective-permute-done((bf16[4,128,512]{2,1,0:T(8,128)(2,1)S(1)}, bf16[4,128,512]{2,1,0:T(8,128)(2,1)S(1)}, u32[]{:S(2)}, u32[]{:S(2)}) %collective-permute-start.34) | collective-permute-done | bytes 524320 | tf_op jit(solution)/shard_map/ppermute | solution.py:152
  230.4 9.5 %collective-permute-done.26 = bf16[4,128,512]{2,1,0:T(8,128)(2,1)S(1)} collective-permute-done((bf16[4,128,512]{2,1,0:T(8,128)(2,1)S(1)}, bf16[4,128,512]{2,1,0:T(8,128)(2,1)S(1)}, u32[]{:S(2)}, u32[]{:S(2)}) %collective-permute-start.26) | collective-permute-done | bytes 524320 | tf_op jit(solution)/shard_map/ppermute | solution.py:152
  239.9 5.3 %collective-permute-start.43 = (bf16[128,512]{1,0:T(8,128)(2,1)S(1)}, bf16[128,512]{1,0:T(8,128)(2,1)S(1)}, u32[]{:S(2)}, u32[]{:S(2)}) collective-permute-start(bf16[128,512]{1,0:T(8,128)(2,1)S(1)} %get-tuple-element.76), channel_id=1, source_target_pairs={{0,4},{1,5},{2,6},{3,7},{16,20},{17,21},{18,22},{19,23}} | collective-permute-start | bytes 393224 | tf_op jit(solution)/shard_map/ppermute | solution.py:162
  258.1 5.0 %collective-permute-start.44 = (bf16[128,512]{1,0:T(8,128)(2,1)S(1)}, bf16[128,512]{1,0:T(8,128)(2,1)S(1)}, u32[]{:S(2)}, u32[]{:S(2)}) collective-permute-start(bf16[128,512]{1,0:T(8,128)(2,1)S(1)} %get-tuple-element.74), channel_id=1, source_target_pairs={{0,4},{1,5},{2,6},{3,7},{4,8},{5,9},{6,10},{7,11},{16,20},{17,21},... | collective-permute-start | bytes 393224 | tf_op jit(solution)/shard_map/ppermute | solution.py:162
  263.9 5.3 %collective-permute-start.36 = (bf16[128,512]{1,0:T(8,128)(2,1)S(1)}, bf16[128,512]{1,0:T(8,128)(2,1)S(1)}, u32[]{:S(2)}, u32[]{:S(2)}) collective-permute-start(bf16[128,512]{1,0:T(8,128)(2,1)S(1)} %get-tuple-element.68), channel_id=1, source_target_pairs={{0,4},{1,5},{2,6},{3,7},{4,8},{5,9},{6,10},{7,11},{16,20},{17,21},... | collective-permute-start | bytes 393224 | tf_op jit(solution)/shard_map/ppermute | solution.py:162
  270.0 5.0 %collective-permute-start.28 = (bf16[128,512]{1,0:T(8,128)(2,1)S(1)}, bf16[128,512]{1,0:T(8,128)(2,1)S(1)}, u32[]{:S(2)}, u32[]{:S(2)}) collective-permute-start(bf16[128,512]{1,0:T(8,128)(2,1)S(1)} %get-tuple-element.62), channel_id=1, source_target_pairs={{0,4},{1,5},{2,6},{3,7},{4,8},{5,9},{6,10},{7,11},{16,20},{17,21},... | collective-permute-start | bytes 393224 | tf_op jit(solution)/shard_map/ppermute | solution.py:162
  278.9 5.1 %collective-permute-start.53 = (bf16[128,512]{1,0:T(8,128)(2,1)S(1)}, bf16[128,512]{1,0:T(8,128)(2,1)S(1)}, u32[]{:S(2)}, u32[]{:S(2)}) collective-permute-start(bf16[128,512]{1,0:T(8,128)(2,1)S(1)} %get-tuple-element.78), channel_id=1, source_target_pairs={{0,4},{1,5},{2,6},{3,7},{4,8},{5,9},{6,10},{7,11},{8,12},{9,13},{1... | collective-permute-start | bytes 393224 | tf_op jit(solution)/shard_map/ppermute | solution.py:162
  322.3 13.6 %collective-permute-done.65 = bf16[128,2048]{1,0:T(8,128)(2,1)S(1)} collective-permute-done((bf16[128,2048]{1,0:T(8,128)(2,1)S(1)}, bf16[128,2048]{1,0:T(8,128)(2,1)S(1)}, u32[]{:S(2)}, u32[]{:S(2)}) %collective-permute-start.65) | collective-permute-done | bytes 524320 | tf_op jit(solution)/shard_map/ppermute | solution.py:162
  342.0 5.2 %collective-permute-done.66 = bf16[128,2048]{1,0:T(8,128)(2,1)S(1)} collective-permute-done((bf16[128,2048]{1,0:T(8,128)(2,1)S(1)}, bf16[128,2048]{1,0:T(8,128)(2,1)S(1)}, u32[]{:S(2)}, u32[]{:S(2)}) %collective-permute-start.66) | collective-permute-done | bytes 524320 | tf_op jit(solution)/shard_map/ppermute | solution.py:162
  348.5 5.3 %collective-permute-done.64 = bf16[128,2048]{1,0:T(8,128)(2,1)S(1)} collective-permute-done((bf16[128,2048]{1,0:T(8,128)(2,1)S(1)}, bf16[128,2048]{1,0:T(8,128)(2,1)S(1)}, u32[]{:S(2)}, u32[]{:S(2)}) %collective-permute-start.64) | collective-permute-done | bytes 524320 | tf_op jit(solution)/shard_map/ppermute | solution.py:162
  361.0 8.9 %collective-permute-done.69 = bf16[128,2048]{1,0:T(8,128)(2,1)S(1)} collective-permute-done((bf16[128,2048]{1,0:T(8,128)(2,1)S(1)}, bf16[128,2048]{1,0:T(8,128)(2,1)S(1)}, u32[]{:S(2)}, u32[]{:S(2)}) %collective-permute-start.69) | collective-permute-done | bytes 524320 | tf_op jit(solution)/shard_map/ppermute | solution.py:156
  380.0 19.5 %collective-permute-done.74 = bf16[128,2048]{1,0:T(8,128)(2,1)S(1)} collective-permute-done((bf16[128,2048]{1,0:T(8,128)(2,1)S(1)}, bf16[128,2048]{1,0:T(8,128)(2,1)S(1)}, u32[]{:S(2)}, u32[]{:S(2)}) %collective-permute-start.74) | collective-permute-done | bytes 524320 | tf_op jit(solution)/shard_map/ppermute | solution.py:156
  410.2 5.8 %collective-permute-done.63 = bf16[320,768]{1,0:T(8,128)(2,1)S(1)} collective-permute-done((bf16[320,768]{1,0:T(8,128)(2,1)S(1)}, bf16[320,768]{1,0:T(8,128)(2,1)S(1)}, u32[]{:S(2)}, u32[]{:S(2)}) %collective-permute-start.63) | collective-permute-done | bytes 491552 | tf_op jit(solution)/shard_map/ppermute | solution.py:22
  416.6 10.0 %collective-permute-done.71 = bf16[320,768]{1,0:T(8,128)(2,1)S(1)} collective-permute-done((bf16[320,768]{1,0:T(8,128)(2,1)S(1)}, bf16[320,768]{1,0:T(8,128)(2,1)S(1)}, u32[]{:S(2)}, u32[]{:S(2)}) %collective-permute-start.71) | collective-permute-done | bytes 491552 | tf_op jit(solution)/shard_map/ppermute | solution.py:22
  427.1 9.6 %collective-permute-done.76 = bf16[320,768]{1,0:T(8,128)(2,1)S(1)} collective-permute-done((bf16[320,768]{1,0:T(8,128)(2,1)S(1)}, bf16[320,768]{1,0:T(8,128)(2,1)S(1)}, u32[]{:S(2)}, u32[]{:S(2)}) %collective-permute-start.76) | collective-permute-done | bytes 491552 | tf_op jit(solution)/shard_map/ppermute | solution.py:22
  440.9 8.9 %fusion.1 = bf16[1,768,2048]{2,1,0:T(8,128)(2,1)} fusion(bf16[2048,2048]{1,0:T(8,128)(2,1)S(1)} %constant_dynamic-update-slice_fusion, f32[2048]{0:T(1024)S(1)} %bitcast.254, bf16[512,768]{1,0:T(8,128)(2,1)S(1)} %bitcast.283, bf16[512,768]{1,0:T(8,128)(2,1)S(1)} %bitcast.288, bf16[512,768]{1,0:T(8,128)(2,1)S(1)} %bitcast.293, bf16[512,768]{1,0:T(8,128)(2,1)S(1)} %bitcast.298), kind=kOutput, calls=%fused_computation.13 | convolution fusion | flops 6459752448 | bytes 14688256 | tf_op jit(solution)/shard_map/dot_general | solution.py:14
  452.9 6.2 %fusion.2 = bf16[1,2048,768]{2,1,0:T(8,128)(2,1)} fusion(bf16[320,768]{1,0:T(8,128)(2,1)S(1)} %get-tuple-element.49, bf16[320,768]{1,0:T(8,128)(2,1)S(1)} %get-tuple-element.47, bf16[320,768]{1,0:T(8,128)(2,1)S(1)} %get-tuple-element.45, bf16[320,768]{1,0:T(8,128)(2,1)S(1)} %get-tuple-element.43, bf16[320,2048]{1,0:T(8,128)(2,1)S(1)} %bitcast.274, ...), kind=kOutput, calls=%fused_computation.14 | convolution fusion | flops 4056940544 | bytes 10354688 | tf_op jit(solution)/shard_map/dot_general | solution.py:14
  459.1 6.2 %fusion.3 = bf16[1,2048,768]{2,1,0:T(8,128)(2,1)} fusion(bf16[320,768]{1,0:T(8,128)(2,1)S(1)} %get-tuple-element.48, bf16[320,768]{1,0:T(8,128)(2,1)S(1)} %get-tuple-element.46, bf16[320,768]{1,0:T(8,128)(2,1)S(1)} %get-tuple-element.44, bf16[320,768]{1,0:T(8,128)(2,1)S(1)} %get-tuple-element.42, bf16[320,2048]{1,0:T(8,128)(2,1)S(1)} %bitcast.275, ...), kind=kOutput, calls=%fused_computation.15 | convolution fusion | flops 4056940544 | bytes 10354688 | tf_op jit(solution)/shard_map/dot_general | solution.py:14
  (349 shorter events, 191.0 us)
Async XLA Ops:
  3.6 21.0 %collective-permute-start.4 = (bf16[128,2048]{1,0:T(8,128)(2,1)}, bf16[128,2048]{1,0:T(8,128)(2,1)}, u32[]{:S(2)}, u32[]{:S(2)}) collective-permute-start(bf16[128,2048]{1,0:T(8,128)(2,1)} %param.7), channel_id=1, source_target_pairs={{0,4},{1,5},{2,6},{3,7},{4,8},{5,9},{6,10},{7,11},{8,12},{9,13},{1... | collective-permute-start | bytes 1572872 | tf_op jit(solution)/shard_map/ppermute | solution.py:162
  7.9 18.2 %collective-permute-start.5 = (bf16[128,2048]{1,0:T(8,128)(2,1)}, bf16[128,2048]{1,0:T(8,128)(2,1)S(1)}, u32[]{:S(2)}, u32[]{:S(2)}) collective-permute-start(bf16[128,2048]{1,0:T(8,128)(2,1)} %param.7), channel_id=1, source_target_pairs={{4,0},{5,1},{6,2},{7,3},{8,4},{9,5},{10,6},{11,7},{12,8},{13,9},{1... | collective-permute-start | bytes 1572872 | tf_op jit(solution)/shard_map/ppermute | solution.py:162
  16.9 35.5 %collective-permute-start.1 = (bf16[256,2048]{1,0:T(8,128)(2,1)S(1)}, bf16[256,2048]{1,0:T(8,128)(2,1)}, u32[]{:S(2)}, u32[]{:S(2)}) collective-permute-start(bf16[256,2048]{1,0:T(8,128)(2,1)S(1)} %pad_maximum_fusion.7), channel_id=1, source_target_pairs={{0,1},{1,0},{2,3},{3,2},{4,5},{5,4},{6,7},{7,6},{8,9},{9,8},{10,11... | collective-permute-start | bytes 3145736 | tf_op jit(solution)/shard_map/ppermute | solution.py:152
  26.1 18.6 %collective-permute-start.6 = (bf16[128,2048]{1,0:T(8,128)(2,1)S(1)}, bf16[128,2048]{1,0:T(8,128)(2,1)}, u32[]{:S(2)}, u32[]{:S(2)}) collective-permute-start(bf16[128,2048]{1,0:T(8,128)(2,1)S(1)} %collective-permute-done.5), channel_id=1, source_target_pairs={{4,0},{5,1},{6,2},{7,3},{8,4},{9,5},{10,6},{11,7},{20,16},{21,17},... | collective-permute-start | bytes 1572872 | tf_op jit(solution)/shard_map/ppermute | solution.py:162
  31.7 28.7 %collective-permute-start.14 = (bf16[128,2048]{1,0:T(8,128)(2,1)}, bf16[128,2048]{1,0:T(8,128)(2,1)S(1)}, u32[]{:S(2)}, u32[]{:S(2)}) collective-permute-start(bf16[128,2048]{1,0:T(8,128)(2,1)} %collective-permute-done.13), channel_id=1, source_target_pairs={{8,10},{9,11},{10,8},{11,9},{12,14},{13,15},{14,12},{15,13},{24,26... | collective-permute-start | bytes 1572872 | tf_op jit(solution)/shard_map/ppermute | solution.py:156
  44.7 15.7 %collective-permute-start.15 = (bf16[128,2048]{1,0:T(8,128)(2,1)}, bf16[128,2048]{1,0:T(8,128)(2,1)S(1)}, u32[]{:S(2)}, u32[]{:S(2)}) collective-permute-start(bf16[128,2048]{1,0:T(8,128)(2,1)} %collective-permute-done.6), channel_id=1, source_target_pairs={{0,2},{1,3},{2,0},{3,1},{4,6},{5,7},{6,4},{7,5},{16,18},{17,19},{1... | collective-permute-start | bytes 1572872 | tf_op jit(solution)/shard_map/ppermute | solution.py:156
  60.6 18.4 %collective-permute-start.16 = (bf16[256,2048]{1,0:T(8,128)(2,1)S(1)}, bf16[256,2048]{1,0:T(8,128)(2,1)}, u32[]{:S(2)}, u32[]{:S(2)}) collective-permute-start(bf16[256,2048]{1,0:T(8,128)(2,1)S(1)} %pad_maximum_fusion.9), channel_id=1, source_target_pairs={{0,1},{1,0},{2,3},{3,2},{4,5},{5,4},{6,7},{7,6},{8,9},{9,8},{10,11... | collective-permute-start | bytes 3145736 | tf_op jit(solution)/shard_map/ppermute | solution.py:152
  60.7 16.7 %collective-permute-start.21 = (bf16[128,2048]{1,0:T(8,128)(2,1)S(1)}, bf16[128,2048]{1,0:T(8,128)(2,1)}, u32[]{:S(2)}, u32[]{:S(2)}) collective-permute-start(bf16[128,2048]{1,0:T(8,128)(2,1)S(1)} %copy-done.6), channel_id=1, source_target_pairs={{0,2},{1,3},{2,0},{3,1},{4,6},{5,7},{6,4},{7,5},{8,10},{9,11},{10,... | collective-permute-start | bytes 1572872 | tf_op jit(solution)/shard_map/ppermute | solution.py:156
  66.5 21.3 %collective-permute-start.8 = (bf16[128,2048]{1,0:T(8,128)(2,1)}, bf16[128,2048]{1,0:T(8,128)(2,1)S(1)}, u32[]{:S(2)}, u32[]{:S(2)}) collective-permute-start(bf16[128,2048]{1,0:T(8,128)(2,1)} %collective-permute-done.4), channel_id=1, source_target_pairs={{4,6},{5,7},{6,4},{7,5},{8,10},{9,11},{10,8},{11,9},{12,14},{13,15... | collective-permute-start | bytes 1572872 | tf_op jit(solution)/shard_map/ppermute | solution.py:156
  71.1 17.7 %collective-permute-start.9 = (bf16[128,2048]{1,0:T(8,128)(2,1)}, bf16[128,2048]{1,0:T(8,128)(2,1)S(1)}, u32[]{:S(2)}, u32[]{:S(2)}) collective-permute-start(bf16[128,2048]{1,0:T(8,128)(2,1)} %collective-permute-done.7), channel_id=1, source_target_pairs={{0,2},{1,3},{2,0},{3,1},{16,18},{17,19},{18,16},{19,17}} | collective-permute-start | bytes 1572872 | tf_op jit(solution)/shard_map/ppermute | solution.py:156
  78.9 22.1 %collective-permute-start.22 = (bf16[256,2048]{1,0:T(8,128)(2,1)S(1)}, bf16[256,2048]{1,0:T(8,128)(2,1)S(1)}, u32[]{:S(2)}, u32[]{:S(2)}) collective-permute-start(bf16[256,2048]{1,0:T(8,128)(2,1)S(1)} %pad_maximum_fusion.10), channel_id=1, source_target_pairs={{0,1},{1,0},{2,3},{3,2},{4,5},{5,4},{6,7},{7,6},{8,9},{9,8},{10,11... | collective-permute-start | bytes 3145736 | tf_op jit(solution)/shard_map/ppermute | solution.py:152
  86.7 78.1 %collective-permute-start.3 = (bf16[160,768]{1,0:T(8,128)(2,1)S(1)}, bf16[160,768]{1,0:T(8,128)(2,1)S(1)}, u32[]{:S(2)}, u32[]{:S(2)}) collective-permute-start(bf16[160,768]{1,0:T(8,128)(2,1)S(1)} %fusion.97), channel_id=1, source_target_pairs={{0,16},{16,0},{1,17},{17,1},{2,18},{18,2},{3,19},{19,3},{4,20},{20... | collective-permute-start | bytes 737288 | tf_op jit(solution)/shard_map/ppermute | solution.py:22
  87.7 221.5 %collective-permute-start.57 = (bf16[160,1536]{1,0:T(8,128)(2,1)S(1)}, bf16[160,1536]{1,0:T(8,128)(2,1)S(1)}, u32[]{:S(2)}, u32[]{:S(2)}) collective-permute-start(bf16[160,1536]{1,0:T(8,128)(2,1)S(1)} %get-tuple-element.38), channel_id=1, source_target_pairs={{0,16},{16,0},{1,17},{17,1},{2,18},{18,2},{3,19},{19,3},{4,20},{20... | collective-permute-start | bytes 1474568 | tf_op jit(solution)/shard_map/ppermute | solution.py:22
  89.1 16.9 %collective-permute-start.10 = (bf16[256,2048]{1,0:T(8,128)(2,1)S(1)}, bf16[256,2048]{1,0:T(8,128)(2,1)S(1)}, u32[]{:S(2)}, u32[]{:S(2)}) collective-permute-start(bf16[256,2048]{1,0:T(8,128)(2,1)S(1)} %pad_maximum_fusion.8), channel_id=1, source_target_pairs={{0,1},{1,0},{2,3},{3,2},{4,5},{5,4},{6,7},{7,6},{8,9},{9,8},{10,11... | collective-permute-start | bytes 3145736 | tf_op jit(solution)/shard_map/ppermute | solution.py:152
  99.9 56.2 %collective-permute-start.18 = (bf16[160,768]{1,0:T(8,128)(2,1)S(1)}, bf16[160,768]{1,0:T(8,128)(2,1)S(1)}, u32[]{:S(2)}, u32[]{:S(2)}) collective-permute-start(bf16[160,768]{1,0:T(8,128)(2,1)S(1)} %fusion.95), channel_id=1, source_target_pairs={{0,16},{16,0},{1,17},{17,1},{2,18},{18,2},{3,19},{19,3},{4,20},{20... | collective-permute-start | bytes 737288 | tf_op jit(solution)/shard_map/ppermute | solution.py:22
  101.0 208.3 %collective-permute-start.59 = (bf16[160,1536]{1,0:T(8,128)(2,1)S(1)}, bf16[160,1536]{1,0:T(8,128)(2,1)S(1)}, u32[]{:S(2)}, u32[]{:S(2)}) collective-permute-start(bf16[160,1536]{1,0:T(8,128)(2,1)S(1)} %get-tuple-element.34), channel_id=1, source_target_pairs={{0,16},{16,0},{1,17},{17,1},{2,18},{18,2},{3,19},{19,3},{4,20},{20... | collective-permute-start | bytes 1474568 | tf_op jit(solution)/shard_map/ppermute | solution.py:22
  105.9 35.7 %collective-permute-start.23 = (bf16[160,1536]{1,0:T(8,128)(2,1)S(1)}, bf16[160,1536]{1,0:T(8,128)(2,1)S(1)}, u32[]{:S(2)}, u32[]{:S(2)}) collective-permute-start(bf16[160,1536]{1,0:T(8,128)(2,1)S(1)} %constant_dynamic-slice_fusion), channel_id=1, source_target_pairs={{0,16},{16,0},{1,17},{17,1},{2,18},{18,2},{3,19},{19,3},{4,20},{20... | collective-permute-start | bytes 1474568 | tf_op jit(solution)/shard_map/ppermute | solution.py:22
  193.7 24.6 %collective-permute-start.42 = (bf16[4,128,512]{2,1,0:T(8,128)(2,1)S(1)}, bf16[4,128,512]{2,1,0:T(8,128)(2,1)S(1)}, u32[]{:S(2)}, u32[]{:S(2)}) collective-permute-start(bf16[4,128,512]{2,1,0:T(8,128)(2,1)S(1)} %slice_bitcast_fusion.2), channel_id=1, source_target_pairs={{0,2},{1,3},{2,0},{3,1},{4,6},{5,7},{6,4},{7,5},{8,10},{9,11},{10,... | collective-permute-start | bytes 1572872 | tf_op jit(solution)/shard_map/ppermute | solution.py:152
  195.2 34.4 %collective-permute-start.34 = (bf16[4,128,512]{2,1,0:T(8,128)(2,1)S(1)}, bf16[4,128,512]{2,1,0:T(8,128)(2,1)S(1)}, u32[]{:S(2)}, u32[]{:S(2)}) collective-permute-start(bf16[4,128,512]{2,1,0:T(8,128)(2,1)S(1)} %slice_bitcast_fusion.4), channel_id=1, source_target_pairs={{0,2},{1,3},{2,0},{3,1},{4,6},{5,7},{6,4},{7,5},{8,10},{9,11},{10,... | collective-permute-start | bytes 1572872 | tf_op jit(solution)/shard_map/ppermute | solution.py:152
  207.1 32.8 %collective-permute-start.26 = (bf16[4,128,512]{2,1,0:T(8,128)(2,1)S(1)}, bf16[4,128,512]{2,1,0:T(8,128)(2,1)S(1)}, u32[]{:S(2)}, u32[]{:S(2)}) collective-permute-start(bf16[4,128,512]{2,1,0:T(8,128)(2,1)S(1)} %slice_bitcast_fusion.6), channel_id=1, source_target_pairs={{0,2},{1,3},{2,0},{3,1},{4,6},{5,7},{6,4},{7,5},{8,10},{9,11},{10,... | collective-permute-start | bytes 1572872 | tf_op jit(solution)/shard_map/ppermute | solution.py:152
  218.3 27.1 %collective-permute-start.51 = (bf16[128,512]{1,0:T(8,128)(2,1)S(1)}, bf16[128,512]{1,0:T(8,128)(2,1)S(1)}, u32[]{:S(2)}, u32[]{:S(2)}) collective-permute-start(bf16[128,512]{1,0:T(8,128)(2,1)S(1)} %get-tuple-element.82), channel_id=1, source_target_pairs={{0,4},{1,5},{2,6},{3,7},{16,20},{17,21},{18,22},{19,23}} | collective-permute-start | bytes 393224 | tf_op jit(solution)/shard_map/ppermute | solution.py:162
  229.5 16.5 %collective-permute-start.54 = (bf16[128,512]{1,0:T(8,128)(2,1)S(1)}, bf16[128,512]{1,0:T(8,128)(2,1)S(1)}, u32[]{:S(2)}, u32[]{:S(2)}) collective-permute-start(bf16[128,512]{1,0:T(8,128)(2,1)S(1)} %get-tuple-element.83), channel_id=1, source_target_pairs={{12,8},{13,9},{14,10},{15,11},{28,24},{29,25},{30,26},{31,27}} | collective-permute-start | bytes 393224 | tf_op jit(solution)/shard_map/ppermute | solution.py:162
  320.4 15.6 %collective-permute-start.65 = (bf16[128,2048]{1,0:T(8,128)(2,1)S(1)}, bf16[128,2048]{1,0:T(8,128)(2,1)S(1)}, u32[]{:S(2)}, u32[]{:S(2)}) collective-permute-start(bf16[128,2048]{1,0:T(8,128)(2,1)S(1)} %get-tuple-element.29), channel_id=1, source_target_pairs={{4,0},{5,1},{6,2},{7,3},{8,4},{9,5},{10,6},{11,7},{12,8},{13,9},{1... | collective-permute-start | bytes 1572872 | tf_op jit(solution)/shard_map/ppermute | solution.py:162
  321.7 15.6 %collective-permute-start.61 = (bf16[128,2048]{1,0:T(8,128)(2,1)S(1)}, bf16[128,2048]{1,0:T(8,128)(2,1)S(1)}, u32[]{:S(2)}, u32[]{:S(2)}) collective-permute-start(bf16[128,2048]{1,0:T(8,128)(2,1)S(1)} %get-tuple-element.29), channel_id=1, source_target_pairs={{0,2},{1,3},{2,0},{3,1},{4,6},{5,7},{6,4},{7,5},{8,10},{9,11},{10,... | collective-permute-start | bytes 1572872 | tf_op jit(solution)/shard_map/ppermute | solution.py:156
  337.4 23.4 %collective-permute-start.62 = (bf16[256,2048]{1,0:T(8,128)(2,1)S(1)}, bf16[256,2048]{1,0:T(8,128)(2,1)S(1)}, u32[]{:S(2)}, u32[]{:S(2)}) collective-permute-start(bf16[256,2048]{1,0:T(8,128)(2,1)S(1)} %pad_maximum_fusion.12), channel_id=1, source_target_pairs={{0,1},{1,0},{2,3},{3,2},{4,5},{5,4},{6,7},{7,6},{8,9},{9,8},{10,11... | collective-permute-start | bytes 3145736 | tf_op jit(solution)/shard_map/ppermute | solution.py:152
  337.4 16.4 %collective-permute-start.64 = (bf16[128,2048]{1,0:T(8,128)(2,1)S(1)}, bf16[128,2048]{1,0:T(8,128)(2,1)S(1)}, u32[]{:S(2)}, u32[]{:S(2)}) collective-permute-start(bf16[128,2048]{1,0:T(8,128)(2,1)S(1)} %get-tuple-element.29), channel_id=1, source_target_pairs={{0,4},{1,5},{2,6},{3,7},{4,8},{5,9},{6,10},{7,11},{8,12},{9,13},{1... | collective-permute-start | bytes 1572872 | tf_op jit(solution)/shard_map/ppermute | solution.py:162
  372.5 34.9 %collective-permute-start.79 = (bf16[128,2048]{1,0:T(8,128)(2,1)S(1)}, bf16[128,2048]{1,0:T(8,128)(2,1)S(1)}, u32[]{:S(2)}, u32[]{:S(2)}) collective-permute-start(bf16[128,2048]{1,0:T(8,128)(2,1)S(1)} %collective-permute-done.65), channel_id=1, source_target_pairs={{0,2},{1,3},{2,0},{3,1},{4,6},{5,7},{6,4},{7,5},{8,10},{9,11},{10,... | collective-permute-start | bytes 1572872 | tf_op jit(solution)/shard_map/ppermute | solution.py:156
  375.0 24.5 %collective-permute-start.74 = (bf16[128,2048]{1,0:T(8,128)(2,1)S(1)}, bf16[128,2048]{1,0:T(8,128)(2,1)S(1)}, u32[]{:S(2)}, u32[]{:S(2)}) collective-permute-start(bf16[128,2048]{1,0:T(8,128)(2,1)S(1)} %collective-permute-done.66), channel_id=1, source_target_pairs={{0,2},{1,3},{2,0},{3,1},{4,6},{5,7},{6,4},{7,5},{16,18},{17,19},{1... | collective-permute-start | bytes 1572872 | tf_op jit(solution)/shard_map/ppermute | solution.py:156
  379.1 23.2 %collective-permute-start.77 = (bf16[128,2048]{1,0:T(8,128)(2,1)S(1)}, bf16[128,2048]{1,0:T(8,128)(2,1)S(1)}, u32[]{:S(2)}, u32[]{:S(2)}) collective-permute-start(bf16[128,2048]{1,0:T(8,128)(2,1)S(1)} %collective-permute-done.72), channel_id=1, source_target_pairs={{8,12},{9,13},{10,14},{11,15},{24,28},{25,29},{26,30},{27,31}} | collective-permute-start | bytes 1572872 | tf_op jit(solution)/shard_map/ppermute | solution.py:162
  405.3 21.2 %collective-permute-start.71 = (bf16[320,768]{1,0:T(8,128)(2,1)S(1)}, bf16[320,768]{1,0:T(8,128)(2,1)S(1)}, u32[]{:S(2)}, u32[]{:S(2)}) collective-permute-start(bf16[320,768]{1,0:T(8,128)(2,1)S(1)} %bitcast.243), channel_id=1, source_target_pairs={{0,16},{16,0},{1,17},{17,1},{2,18},{18,2},{3,19},{19,3},{4,20},{20... | collective-permute-start | bytes 1474568 | tf_op jit(solution)/shard_map/ppermute | solution.py:22
  407.6 29.6 %collective-permute-start.80 = (bf16[256,2048]{1,0:T(8,128)(2,1)S(1)}, bf16[256,2048]{1,0:T(8,128)(2,1)S(1)}, u32[]{:S(2)}, u32[]{:S(2)}) collective-permute-start(bf16[256,2048]{1,0:T(8,128)(2,1)S(1)} %pad_maximum_fusion.15), channel_id=1, source_target_pairs={{0,1},{1,0},{2,3},{3,2},{4,5},{5,4},{6,7},{7,6},{8,9},{9,8},{10,11... | collective-permute-start | bytes 3145736 | tf_op jit(solution)/shard_map/ppermute | solution.py:152
  409.8 26.8 %collective-permute-start.76 = (bf16[320,768]{1,0:T(8,128)(2,1)S(1)}, bf16[320,768]{1,0:T(8,128)(2,1)S(1)}, u32[]{:S(2)}, u32[]{:S(2)}) collective-permute-start(bf16[320,768]{1,0:T(8,128)(2,1)S(1)} %bitcast.244), channel_id=1, source_target_pairs={{0,16},{16,0},{1,17},{17,1},{2,18},{18,2},{3,19},{19,3},{4,20},{20... | collective-permute-start | bytes 1474568 | tf_op jit(solution)/shard_map/ppermute | solution.py:22
  (89 other events, 914.5 us)

commit v3 on v2

--- a/solution.py
+++ b/solution.py
@@ -145,137 +145,101 @@
     return (mixed, grad_gate[None], grad_up[None], grad_down[None])
 
 
-Z = 4
-
-
-def across(value, bit):
-    return lax.ppermute(value, "ep", [(i, i ^ bit) for i in range(4 * Z)])
-
-
-def across_x(value, low, high):
-    return lax.ppermute(
-        value, "ep", [(z * 4 + i, z * 4 + (i ^ 2)) for z in range(low, high) for i in range(4)]
-    )
-
-
-def along_z(value, low, high, step):
-    return lax.ppermute(
-        value,
-        "ep",
-        [(z * 4 + i, (z + step) * 4 + i) for z in range(low, high) for i in range(4)],
-    )
-
-
-def gather_groups(value):
-    up1 = along_z(value, 0, 3, 1)
-    down1 = along_z(value, 1, 4, -1)
-    side0 = across_x(value, 0, 4)
-    up2 = along_z(up1, 1, 3, 1)
-    down2 = along_z(down1, 1, 3, -1)
-    side_up1 = across_x(up1, 1, 4)
-    side_down1 = across_x(down1, 0, 3)
-    up3 = along_z(up2, 2, 3, 1)
-    down3 = along_z(down2, 1, 2, -1)
-    side_up2 = across_x(up2, 2, 4)
-    side_down2 = across_x(down2, 0, 2)
-    side_up3 = across_x(up3, 3, 4)
-    side_down3 = across_x(down3, 0, 1)
-    pairs = [
-        (value, side0),
-        (up1 + down3, side_up1 + side_down3),
-        (up2 + down2, side_up2 + side_down2),
-        (up3 + down1, side_up3 + side_down1),
-    ]
-    groups = []
-    for own, side in pairs:
-        mine = jnp.concatenate([own, side], 0)
-        other = across(mine, 1)
-        groups.append(jnp.concatenate([mine, other], 0))
-    return groups
-
-
-def scatter_sum(value):
-    def add(a, b):
-        return (a.astype(F32) + b.astype(F32)).astype(BF)
-
-    value = add(value[:, 0], across(value[:, 1], 1))
-    value = add(value[:, 0], across(value[:, 1], 2))
-    up = along_z(value[1], 0, 1, 1)
-    down = along_z(value[3], 3, 4, -1)
-    up = along_z(add(value[2], up), 0, 2, 1)
-    down = along_z(add(value[2], down), 2, 4, -1)
-    up = along_z(add(value[3], up), 0, 3, 1)
-    down = along_z(add(value[1], down), 1, 4, -1)
-    return value[0].astype(F32) + up.astype(F32) + down.astype(F32)
-
-
-ORDER = (0, 2, 1, 3)
-CHUNKS = 4
+def across(value):
+    count = lax.axis_size("ep")
+    return lax.ppermute(value, "ep", [(i, i ^ 1) for i in range(count)])
+
+
+def same_core():
+    count = lax.axis_size("ep")
+    return [list(range(core, count, 2)) for core in range(2)]
+
+
+def gather_core(value):
+    return lax.all_gather(value, "ep", axis=0, tiled=True, axis_index_groups=same_core())
+
+
+def with_other_core(mine):
+    half = mine.shape[0] // 2
+    return [mine, across(mine[:half]), across(mine[half:])]
 
 
 def local(signal, routes, gates, pairing, w_gate, w_up, w_down):
     experts = lax.axis_size("ep")
     rank = lax.axis_index("rep")
-    me = lax.axis_index("ep")
+    core = lax.axis_index("ep") % 2
     row_count, width = signal.shape
     capacity = min(row_count, row_count * TOP * 5 // (4 * experts))
     w_gate, w_up, w_down = w_gate[0], w_up[0], w_down[0]
     hidden_width = w_gate.shape[1]
+    half, quarter = experts // 2, experts // 4
+    spans = ((0, half), (half, half + quarter), (half + quarter, experts))
+
+    mine, w_down_other = lax.optimization_barrier((gather_core(signal), across(w_down)))
+    row_groups = with_other_core(mine)
+    w_down_pair = jnp.concatenate([w_down, w_down_other], 0)
     w_both = jnp.concatenate([w_gate, w_up], 1)
-
-    row_groups = gather_groups(signal)
-    weight = gate_table(routes, gates, experts)
-    place = jnp.arange(experts, dtype=jnp.int32)
-    owner = ((me // 4 - place // 4 + Z) % Z) * 4 + (me % 4) ^ (place % 2 * 2 + place // 2 % 2)
-    weight = jnp.take(weight, owner, axis=0)
-    pick = slot_picks(weight, capacity).reshape(Z, 4, capacity, row_count)
-    row_weight = weight.reshape(Z, 4 * row_count, 1)
-
-    arrived, hidden, gate_up, spread = [None] * Z, [None] * Z, [None] * Z, [None] * Z
-    for k in ORDER:
-        rows = row_groups[k].reshape(4, row_count, width)
-        arrived[k] = blocks_mm(pick[k], rows, 2, 1).astype(BF).reshape(4 * capacity, width)
-        own = half_sum(mm(arrived[k], w_both).astype(BF), rank)
+    weight = gate_table(routes, gates, experts).reshape(half, 2, row_count)
+    weight = jnp.where(
+        core == 0,
+        jnp.concatenate([weight[:, 0], weight[:, 1]], 0),
+        jnp.concatenate([weight[:, 1], weight[:, 0]], 0),
+    )
+    pick = slot_picks(weight, capacity)
+    row_weight = weight.reshape(experts * row_count, 1)
+
+    arrived, gate_up, weighted, handed = [], [], [], []
+    for (low, high), rows in zip(spans, row_groups):
+        count = high - low
+        chosen = pick[low:high]
+        arrived.append(
+            blocks_mm(chosen, rows.reshape(count, row_count, width), 2, 1)
+            .astype(BF)
+            .reshape(count * capacity, width)
+        )
+        own = half_sum(mm(arrived[-1], w_both).astype(BF), rank)
         gate, up = own[:, :hidden_width], own[:, hidden_width:]
         hidden_own = (gate * jax.nn.sigmoid(gate) * up).astype(BF)
-        gate_up[k] = own.astype(BF)
-        hidden[k] = both_halves(hidden_own, swap(hidden_own), rank)
-        spread[k] = (
-            blocks_mm(pick[k], hidden[k].reshape(4, capacity, hidden_width), 1, 1)
-            .astype(BF)
-            .reshape(4 * row_count, hidden_width)
-        )
-    spread = jnp.concatenate(spread, 0)
-    all_weight = weight.reshape(experts * row_count, 1)
-
-    part = width // CHUNKS
-    combined = []
-    for c in range(CHUNKS):
-        returned = (mm(spread, w_down[:, c * part : (c + 1) * part]) * all_weight).astype(BF)
-        combined.append(scatter_sum(returned.reshape(Z, 2, 2, row_count, part)))
-    combined = jnp.concatenate(combined, 1)
+        gate_up.append(own.astype(BF))
+        hidden = both_halves(hidden_own, swap(hidden_own), rank)
+        spread = blocks_mm(chosen, hidden.reshape(count, capacity, hidden_width), 1, 1).reshape(
+            count * row_count, hidden_width
+        )
+        weighted.append((spread * row_weight[low * row_count : high * row_count]).astype(BF))
+        if low > 0:
+            handed.append(across(weighted[-1]))
+
+    inner = jnp.concatenate([weighted[0], jnp.concatenate(handed, 0)], 1)
+    returned = mm(inner, w_down_pair).astype(BF)
+    combined = lax.psum_scatter(
+        returned, "ep", scatter_dimension=0, tiled=True, axis_index_groups=same_core()
+    )
     others = [swap(value) for value in gate_up]
     combined, others = lax.optimization_barrier((combined, others))
-    mixed = combined.astype(BF)
-    grad_rows = row_gradient(combined, pairing)
-
-    grad_groups = gather_groups(grad_rows)
-    gate_pre, up_pre = [None] * Z, [None] * Z
-    for k in ORDER:
-        rows = (mm(grad_groups[k], w_down, 1, 1) * row_weight[k]).astype(BF)
+    mixed = combined
+    grad_rows = row_gradient(combined.astype(F32), pairing)
+
+    grad_groups = with_other_core(gather_core(grad_rows))
+    gate_pre, up_pre = [], []
+    for (low, high), rows, own, other in zip(spans, grad_groups, gate_up, others):
+        count = high - low
+        product = (mm(rows, w_down, 1, 1) * row_weight[low * row_count : high * row_count]).astype(BF)
         sent = (
-            blocks_mm(pick[k], rows.reshape(4, row_count, hidden_width), 2, 1)
-            .reshape(4 * capacity, hidden_width)
+            blocks_mm(pick[low:high], product.reshape(count, row_count, hidden_width), 2, 1)
+            .reshape(count * capacity, hidden_width)
             .astype(BF)
         )
         grad_hidden = sent.astype(F32) + swap(sent).astype(F32)
-        both = both_halves(gate_up[k], others[k], rank).astype(F32)
+        both = both_halves(own, other, rank).astype(F32)
         gate, up = both[:, :hidden_width], both[:, hidden_width:]
         sigma = jax.nn.sigmoid(gate)
-        gate_pre[k] = (grad_hidden * up * sigma * (1.0 + gate * (1.0 - sigma))).astype(BF)
-        up_pre[k] = (grad_hidden * gate * sigma).astype(BF)
-    weighted = (spread.astype(F32) * all_weight).astype(BF)
-    grad_down = mm(weighted, jnp.concatenate(grad_groups, 0), 0, 0).astype(BF)
+        gate_pre.append(
+            (grad_hidden * up * sigma * (1.0 + gate * (1.0 - sigma))).astype(BF)
+        )
+        up_pre.append((grad_hidden * gate * sigma).astype(BF))
+    grad_down = mm(
+        jnp.concatenate(weighted, 0), jnp.concatenate(grad_groups, 0), 0, 0
+    ).astype(BF)
     arrived = jnp.concatenate(arrived, 0)
     grad_gate = mm(arrived, jnp.concatenate(gate_pre, 0), 0, 0).astype(BF)
     grad_up = mm(arrived, jnp.concatenate(up_pre, 0), 0, 0).astype(BF)
@@ -283,7 +247,7 @@
 
 
 def solution(mesh):
-    blocked = mesh.shape["ep"] == 4 * Z and mesh.shape["rep"] == 2
+    blocked = mesh.shape["ep"] % 4 == 0 and mesh.shape["rep"] == 2
     return jax.shard_map(
         local if blocked else local_general,
         mesh=mesh,

time: 472 us -> 441 us (0.934)
  starting transfers between devices: 136 us -> 23.2 us
  waiting for transfers between devices: 223 us -> 305 us
  between operations: 3.13 us -> 14.8 us
  matrix products: 68.9 us -> 57.8 us
  local copies, waits for them, and re-layouts: 6.16 us -> 15.8 us
  other arithmetic: 23.3 us -> 13.8 us
    all_gather x0 -> x2, waiting for transfers between devices: none -> 136 us  [gather_core(): lax.all_gather(value, 'ep', axis=0, tiled=True, axis_index_groups=same_co...]
    ppermute x66 -> x7, waiting for transfers between devices: 125 us -> 0.02 us  [across(): return lax.ppermute(value, 'ep', [(i, i ^ 1) for i in range(count)])]
    ppermute x66 -> x7, starting transfers between devices: 115 us -> 1.46 us  [across(): return lax.ppermute(value, 'ep', [(i, i ^ 1) for i in range(count)])]
    reduce_scatter x0 -> x1, waiting for transfers between devices: none -> 42.6 us  [local(): lax.psum_scatter(returned, 'ep', scatter_dimension=0, tiled=True, axis_in...]
    ppermute x16 -> x12, waiting for transfers between devices: 94.8 us -> 119 us  [swap(): return lax.ppermute(value, 'rep', [(0, 1), (1, 0)])]
    dot_general x15 -> x10, matrix products: 62.9 us -> 50 us  [mm(): lax.dot_general(a, b, (((ca,), (cb,)), ((), ())), preferred_element_type=...]
    slice x4 -> x3, local copies, waits for them, and re-layouts: 0.55 us -> 7.66 us  [the longest x2 7.66 us: with_other_core(): return [mine, across(mine[:half]), across(mine[half:])]]
    add x10 -> x0, other arithmetic: 5.7 us -> none  [the longest x1 1.33 us: gather_groups(): up2 + down2]
  transfers between devices with their start and end apart: 83 -> 23, of which waited for: 31 -> 15; matrix products, arithmetic and copies ran while one was open for 16% -> 10% of each run, Pallas kernels for 0% -> 0%
where the time goes in v3:
time: 441 us; the launch traced here: 436 us
  waiting for transfers between devices  305 us (69%)
  matrix products  57.8 us (13%)
  starting transfers between devices  23.2 us (5%)
  local copies, waits for them, and re-layouts  15.8 us (4%)
  between operations  14.8 us (3%)
  other arithmetic  13.8 us (3%)
  blocking collectives  5.15 us (1%)
    all_gather x2, waiting for transfers between devices, gather_core(): lax.all_gather(value, 'ep', axis=0, tiled=True, axis_index_groups=same_co...  136 us
    ppermute x12, waiting for transfers between devices, swap(): return lax.ppermute(value, 'rep', [(0, 1), (1, 0)])  119 us
    dot_general x10, matrix products, mm(): lax.dot_general(a, b, (((ca,), (cb,)), ((), ())), preferred_element_type=...  50 us
    reduce_scatter x1, waiting for transfers between devices, local(): lax.psum_scatter(returned, 'ep', scatter_dimension=0, tiled=True, axis_in...  42.6 us
    ppermute x12, starting transfers between devices, swap(): return lax.ppermute(value, 'rep', [(0, 1), (1, 0)])  14.6 us
  transfers between devices with their start and end apart: 23, of which 15 were waited for; matrix products, arithmetic and copies ran while one was open for 10% of the time, Pallas kernels for 0%

profile of v3, /device:TPU:0, one launch (start us, length us, event | category | flops | bytes accessed | tf_op | source)
XLA Modules:
  0.0 435.5 jit_solution(3027335664992589269)
XLA Ops:
  9.7 7.0 %all-to-all-start = ((f32[16,1,128]{2,1,0:T(1,128)}), f32[16,1,128]{2,1,0:T(1,128)S(1)}, u32[]{:S(2)}, u32[]{:S(2)}) async-start(f32[16,1,128]{2,1,0:T(1,128)} %bitcast.2), calls=%async_computation | async-start | bytes 16384 | tf_op jit(solution)/shard_map/all_to_all | solution.py:81
  16.8 6.3 %all-to-all-done = f32[16,1,128]{2,1,0:T(1,128)S(1)} async-done(((f32[16,1,128]{2,1,0:T(1,128)}), f32[16,1,128]{2,1,0:T(1,128)S(1)}, u32[]{:S(2)}, u32[]{:S(2)}) %all-to-all-start) | async-done | bytes 8224 | tf_op jit(solution)/shard_map/all_to_all | solution.py:81
  23.3 63.1 %all-gather.3.cloned.1.call-done = bf16[1024,2048]{1,0:T(8,128)(2,1)} async-done(((bf16[128,2048]{1,0:T(8,128)(2,1)}), bf16[1024,2048]{1,0:T(8,128)(2,1)}) %all-gather.3.cloned.1.call-update) | async-done | bytes 4194320 | tf_op jit(solution)/shard_map/all_gather | solution.py:159
  86.4 5.0 %fusion.114 = (bf16[512,2048]{1,0:T(8,128)(2,1)}, bf16[512,2048]{1,0:T(8,128)(2,1)}) fusion(bf16[1024,2048]{1,0:T(8,128)(2,1)} %all-gather.3.cloned.1.call-done), kind=kLoop, calls=%fused_computation.169 | loop fusion | bytes 8388608 | tf_op jit(solution)/shard_map/slice | solution.py:164
  93.3 1.8 copy-done.16
  95.1 4.2 convolution_convert_fusion.3
  99.5 1.5 collective-permute-start.1
  101.3 22.5 %collective-permute-done.1 = bf16[320,1536]{1,0:T(8,128)(2,1)} collective-permute-done((bf16[320,1536]{1,0:T(8,128)(2,1)S(1)}, bf16[320,1536]{1,0:T(8,128)(2,1)}, u32[]{:S(2)}, u32[]{:S(2)}) %collective-permute-start.1) | collective-permute-done | bytes 983072 | tf_op jit(solution)/shard_map/ppermute | solution.py:22
  125.4 2.1 convolution_convert_fusion.4
  127.5 3.4 convolution_convert_fusion.6
  134.1 3.2 convolution_convert_fusion.7
  137.9 7.2 %collective-permute-done.8 = bf16[160,1536]{1,0:T(8,128)(2,1)S(1)} collective-permute-done((bf16[160,1536]{1,0:T(8,128)(2,1)S(1)}, bf16[160,1536]{1,0:T(8,128)(2,1)S(1)}, u32[]{:S(2)}, u32[]{:S(2)}) %collective-permute-start.8) | collective-permute-done | bytes 491552 | tf_op jit(solution)/shard_map/ppermute | solution.py:22
  147.0 8.7 %collective-permute-done.4 = bf16[160,1536]{1,0:T(8,128)(2,1)S(1)} collective-permute-done((bf16[160,1536]{1,0:T(8,128)(2,1)S(1)}, bf16[160,1536]{1,0:T(8,128)(2,1)S(1)}, u32[]{:S(2)}, u32[]{:S(2)}) %collective-permute-start.4) | collective-permute-done | bytes 491552 | tf_op jit(solution)/shard_map/ppermute | solution.py:22
  158.5 2.5 collective-permute-done.9
  161.0 5.3 %collective-permute-done.5 = bf16[160,768]{1,0:T(8,128)(2,1)S(1)} collective-permute-done((bf16[160,768]{1,0:T(8,128)(2,1)S(1)}, bf16[160,768]{1,0:T(8,128)(2,1)S(1)}, u32[]{:S(2)}, u32[]{:S(2)}) %collective-permute-start.5) | collective-permute-done | bytes 245792 | tf_op jit(solution)/shard_map/ppermute | solution.py:22
  168.4 7.1 %collective-permute-done.2 = bf16[320,768]{1,0:T(8,128)(2,1)S(1)} collective-permute-done((bf16[320,768]{1,0:T(8,128)(2,1)S(1)}, bf16[320,768]{1,0:T(8,128)(2,1)S(1)}, u32[]{:S(2)}, u32[]{:S(2)}) %collective-permute-start.2) | collective-permute-done | bytes 491552 | tf_op jit(solution)/shard_map/ppermute | solution.py:22
  179.0 9.7 %fusion.10 = bf16[1024,2048]{1,0:T(8,128)(2,1)} fusion(bf16[768,2048]{1,0:T(8,128)(2,1)} %collective-permute-done, bf16[768,2048]{1,0:T(8,128)(2,1)S(1)} %bitcast.98, bf16[512,768]{1,0:T(8,128)(2,1)S(1)} %collective-permute-done.10, bf16[512,768]{1,0:T(8,128)(2,1)S(1)} %collective-permute-done.6, bf16[1024,768]{1,0:T(8,128)(2,1)S(1)} %fusion.26), kind=kOutput, calls=%fused_computation.12 | convolution fusion | flops 6466568192 | bytes 13631488 | tf_op jit(solution)/shard_map/dot_general | solution.py:14
  192.3 21.2 %collective-permute-done.11 = bf16[320,1536]{1,0:T(8,128)(2,1)S(1)} collective-permute-done((bf16[320,1536]{1,0:T(8,128)(2,1)S(1)}, bf16[320,1536]{1,0:T(8,128)(2,1)S(1)}, u32[]{:S(2)}, u32[]{:S(2)}) %collective-permute-start.11) | collective-permute-done | bytes 983072 | tf_op jit(solution)/shard_map/ppermute | solution.py:22
  213.5 10.5 %collective-permute-done.13 = bf16[160,1536]{1,0:T(8,128)(2,1)S(1)} collective-permute-done((bf16[160,1536]{1,0:T(8,128)(2,1)S(1)}, bf16[160,1536]{1,0:T(8,128)(2,1)S(1)}, u32[]{:S(2)}, u32[]{:S(2)}) %collective-permute-start.13) | collective-permute-done | bytes 491552 | tf_op jit(solution)/shard_map/ppermute | solution.py:22
  224.0 8.4 %collective-permute-done.12 = bf16[160,1536]{1,0:T(8,128)(2,1)} collective-permute-done((bf16[160,1536]{1,0:T(8,128)(2,1)S(1)}, bf16[160,1536]{1,0:T(8,128)(2,1)}, u32[]{:S(2)}, u32[]{:S(2)}) %collective-permute-start.12) | collective-permute-done | bytes 491552 | tf_op jit(solution)/shard_map/ppermute | solution.py:22
  232.5 42.6 %reduce-scatter.2.cloned.1.call-done = bf16[128,2048]{1,0:T(8,128)(2,1)} async-done(((bf16[1024,2048]{1,0:T(8,128)(2,1)}), bf16[128,2048]{1,0:T(8,128)(2,1)}) %reduce-scatter.2.cloned.1.call-update) | async-done | bytes 524304 | tf_op jit(solution)/shard_map/reduce_scatter | solution.py:214
  278.8 5.2 %psum.7 = f32[224]{0:T(256)S(1)} all-reduce(f32[224]{0:T(256)S(1)} %pad_maximum_fusion.7), channel_id=1, replica_groups=mesh['rep'=2,'ep'=16] {'rep'}, use_global_device_ids=true, to_apply=%region_4.5 | all-reduce | flops 224 | bytes 1792 | tf_op jit(solution)/shard_map/psum | solution.py:50
  286.4 73.3 %all-gather.5.cloned.1.call-done = bf16[1024,2048]{1,0:T(8,128)(2,1)} async-done(((bf16[128,2048]{1,0:T(8,128)(2,1)}), bf16[1024,2048]{1,0:T(8,128)(2,1)}) %all-gather.5.cloned.1.call-update) | async-done | bytes 4194320 | tf_op jit(solution)/shard_map/all_gather | solution.py:159
  359.7 2.7 fusion.113
  364.1 3.4 multiply_convert_fusion
  371.9 18.7 %collective-permute-done.14 = bf16[640,768]{1,0:T(8,128)(2,1)S(1)} collective-permute-done((bf16[640,768]{1,0:T(8,128)(2,1)S(1)}, bf16[640,768]{1,0:T(8,128)(2,1)S(1)}, u32[]{:S(2)}, u32[]{:S(2)}) %collective-permute-start.14) | collective-permute-done | bytes 983072 | tf_op jit(solution)/shard_map/ppermute | solution.py:22
  391.7 1.8 multiply_convert_fusion.3
  395.4 1.8 multiply_convert_fusion.2
  398.2 10.0 %fusion.27 = bf16[1,768,2048]{2,1,0:T(8,128)(2,1)} fusion(bf16[512,2048]{1,0:T(8,128)(2,1)} %copy-done.21, bf16[512,2048]{1,0:T(8,128)(2,1)} %copy-done.20, bf16[1024,2048]{1,0:T(8,128)(2,1)S(1)} %copy-done.2, bf16[512,768]{1,0:T(8,128)(2,1)S(1)} %copy-done.10, bf16[512,768]{1,0:T(8,128)(2,1)S(1)} %copy-done.8, bf16[1024,768]{1,0:T(8,128)(2,1)S(1)} %copy-done.4), kind=kOutput, calls=%fused_computation.31 | convolution fusion | flops 6478626816 | bytes 14680064 | tf_op jit(solution)/shard_map/dot_general | solution.py:14
  408.8 6.8 %collective-permute-done.18 = bf16[320,768]{1,0:T(8,128)(2,1)S(1)} collective-permute-done((bf16[320,768]{1,0:T(8,128)(2,1)S(1)}, bf16[320,768]{1,0:T(8,128)(2,1)S(1)}, u32[]{:S(2)}, u32[]{:S(2)}) %collective-permute-start.18) | collective-permute-done | bytes 491552 | tf_op jit(solution)/shard_map/ppermute | solution.py:22
  416.1 6.2 %fusion.33 = bf16[1,2048,768]{2,1,0:T(8,128)(2,1)} fusion(bf16[320,2048]{1,0:T(8,128)(2,1)S(1)} %bitcast.105, bf16[320,2048]{1,0:T(8,128)(2,1)S(1)} %bitcast.108, bf16[640,2048]{1,0:T(8,128)(2,1)S(1)} %bitcast.101, bf16[320,768]{1,0:T(8,128)(2,1)S(1)} %get-tuple-element.36, bf16[320,768]{1,0:T(8,128)(2,1)S(1)} %get-tuple-element.34, ...), kind=kOutput, calls=%fused_computation.33 | convolution fusion | flops 4049731584 | bytes 10354688 | tf_op jit(solution)/shard_map/dot_general | solution.py:14
  422.4 6.2 %fusion.32 = bf16[1,2048,768]{2,1,0:T(8,128)(2,1)} fusion(bf16[320,2048]{1,0:T(8,128)(2,1)S(1)} %bitcast.106, bf16[320,2048]{1,0:T(8,128)(2,1)S(1)} %bitcast.109, bf16[640,2048]{1,0:T(8,128)(2,1)S(1)} %bitcast.102, bf16[320,768]{1,0:T(8,128)(2,1)S(1)} %get-tuple-element.37, bf16[320,768]{1,0:T(8,128)(2,1)S(1)} %get-tuple-element.35, ...), kind=kOutput, calls=%fused_computation.32 | convolution fusion | flops 4049731584 | bytes 10354688 | tf_op jit(solution)/shard_map/dot_general | solution.py:14
  (137 shorter events, 41.2 us)
Async XLA Ops:
  7.2 79.2 %all-gather.3.cloned.1.call-start = ((), (), s32[]{:S(2)}) async-start(), calls=%async_computation.2 | async-start | bytes 4718592 | tf_op jit(solution)/shard_map/all_gather | solution.py:159
  7.9 15.4 %collective-permute-start = (bf16[768,2048]{1,0:T(8,128)(2,1)}, bf16[768,2048]{1,0:T(8,128)(2,1)}, u32[]{:S(2)}, u32[]{:S(2)}) collective-permute-start(bf16[768,2048]{1,0:T(8,128)(2,1)} %bitcast.97), channel_id=1, source_target_pairs={{0,1},{1,0},{2,3},{3,2},{4,5},{5,4},{6,7},{7,6},{8,9},{9,8},{10,11... | collective-permute-start | bytes 9437192 | tf_op jit(solution)/shard_map/ppermute | solution.py:150
  9.7 13.4 %all-to-all-start = ((f32[16,1,128]{2,1,0:T(1,128)}), f32[16,1,128]{2,1,0:T(1,128)S(1)}, u32[]{:S(2)}, u32[]{:S(2)}) async-start(f32[16,1,128]{2,1,0:T(1,128)} %bitcast.2), calls=%async_computation | async-start | bytes 16384 | tf_op jit(solution)/shard_map/all_to_all | solution.py:81
  16.8 258.3 %reduce-scatter.2.cloned.1.call-start = ((), (), s32[]{:S(2)}) async-start(), calls=%async_computation.3 | async-start | bytes 4718592 | tf_op jit(solution)/shard_map/reduce_scatter | solution.py:214
  91.3 34.0 %collective-permute-start.7 = (bf16[512,2048]{1,0:T(8,128)(2,1)}, bf16[512,2048]{1,0:T(8,128)(2,1)}, u32[]{:S(2)}, u32[]{:S(2)}) collective-permute-start(bf16[512,2048]{1,0:T(8,128)(2,1)} %get-tuple-element.33), channel_id=1, source_target_pairs={{0,1},{1,0},{2,3},{3,2},{4,5},{5,4},{6,7},{7,6},{8,9},{9,8},{10,11... | collective-permute-start | bytes 6291464 | tf_op jit(solution)/shard_map/ppermute | solution.py:150
  99.5 24.3 %collective-permute-start.1 = (bf16[320,1536]{1,0:T(8,128)(2,1)S(1)}, bf16[320,1536]{1,0:T(8,128)(2,1)}, u32[]{:S(2)}, u32[]{:S(2)}) collective-permute-start(bf16[320,1536]{1,0:T(8,128)(2,1)S(1)} %constant_dynamic-slice_fusion.2), channel_id=1, source_target_pairs={{0,16},{16,0},{1,17},{17,1},{2,18},{18,2},{3,19},{19,3},{4,20},{20... | collective-permute-start | bytes 2949128 | tf_op jit(solution)/shard_map/ppermute | solution.py:22
  101.0 31.5 %collective-permute-start.3 = (bf16[512,2048]{1,0:T(8,128)(2,1)}, bf16[512,2048]{1,0:T(8,128)(2,1)S(1)}, u32[]{:S(2)}, u32[]{:S(2)}) collective-permute-start(bf16[512,2048]{1,0:T(8,128)(2,1)} %get-tuple-element.32), channel_id=1, source_target_pairs={{0,1},{1,0},{2,3},{3,2},{4,5},{5,4},{6,7},{7,6},{8,9},{9,8},{10,11... | collective-permute-start | bytes 6291464 | tf_op jit(solution)/shard_map/ppermute | solution.py:150
  101.3 26.2 %copy-start.15 = (bf16[1,2048,768]{2,1,0:T(8,128)(2,1)S(1)}, bf16[1,2048,768]{2,1,0:T(8,128)(2,1)}, u32[]{:S(2)}) copy-start(bf16[1,2048,768]{2,1,0:T(8,128)(2,1)} %param.12) | copy-start | bytes 9437188
  101.3 26.2 %copy-start.17 = (bf16[1,2048,768]{2,1,0:T(8,128)(2,1)S(1)}, bf16[1,2048,768]{2,1,0:T(8,128)(2,1)}, u32[]{:S(2)}) copy-start(bf16[1,2048,768]{2,1,0:T(8,128)(2,1)} %param.11) | copy-start | bytes 9437188
  131.0 14.2 %collective-permute-start.8 = (bf16[160,1536]{1,0:T(8,128)(2,1)S(1)}, bf16[160,1536]{1,0:T(8,128)(2,1)S(1)}, u32[]{:S(2)}, u32[]{:S(2)}) collective-permute-start(bf16[160,1536]{1,0:T(8,128)(2,1)S(1)} %constant_dynamic-slice_fusion), channel_id=1, source_target_pairs={{0,16},{16,0},{1,17},{17,1},{2,18},{18,2},{3,19},{19,3},{4,20},{20... | collective-permute-start | bytes 1474568 | tf_op jit(solution)/shard_map/ppermute | solution.py:22
  137.3 18.4 %collective-permute-start.4 = (bf16[160,1536]{1,0:T(8,128)(2,1)S(1)}, bf16[160,1536]{1,0:T(8,128)(2,1)S(1)}, u32[]{:S(2)}, u32[]{:S(2)}) collective-permute-start(bf16[160,1536]{1,0:T(8,128)(2,1)S(1)} %constant_dynamic-slice_fusion.1), channel_id=1, source_target_pairs={{0,16},{16,0},{1,17},{17,1},{2,18},{18,2},{3,19},{19,3},{4,20},{20... | collective-permute-start | bytes 1474568 | tf_op jit(solution)/shard_map/ppermute | solution.py:22
  145.5 15.5 %collective-permute-start.9 = (bf16[160,768]{1,0:T(8,128)(2,1)S(1)}, bf16[160,768]{1,0:T(8,128)(2,1)S(1)}, u32[]{:S(2)}, u32[]{:S(2)}) collective-permute-start(bf16[160,768]{1,0:T(8,128)(2,1)S(1)} %fusion.76), channel_id=1, source_target_pairs={{0,16},{16,0},{1,17},{17,1},{2,18},{18,2},{3,19},{19,3},{4,20},{20... | collective-permute-start | bytes 737288 | tf_op jit(solution)/shard_map/ppermute | solution.py:22
  156.0 10.2 %collective-permute-start.5 = (bf16[160,768]{1,0:T(8,128)(2,1)S(1)}, bf16[160,768]{1,0:T(8,128)(2,1)S(1)}, u32[]{:S(2)}, u32[]{:S(2)}) collective-permute-start(bf16[160,768]{1,0:T(8,128)(2,1)S(1)} %fusion.77), channel_id=1, source_target_pairs={{0,16},{16,0},{1,17},{17,1},{2,18},{18,2},{3,19},{19,3},{4,20},{20... | collective-permute-start | bytes 737288 | tf_op jit(solution)/shard_map/ppermute | solution.py:22
  157.8 17.6 %collective-permute-start.2 = (bf16[320,768]{1,0:T(8,128)(2,1)S(1)}, bf16[320,768]{1,0:T(8,128)(2,1)S(1)}, u32[]{:S(2)}, u32[]{:S(2)}) collective-permute-start(bf16[320,768]{1,0:T(8,128)(2,1)S(1)} %fusion.59), channel_id=1, source_target_pairs={{0,16},{16,0},{1,17},{17,1},{2,18},{18,2},{3,19},{19,3},{4,20},{20... | collective-permute-start | bytes 1474568 | tf_op jit(solution)/shard_map/ppermute | solution.py:22
  167.2 8.7 %copy-start.7 = (bf16[512,768]{1,0:T(8,128)(2,1)}, bf16[512,768]{1,0:T(8,128)(2,1)S(1)}, u32[]{:S(2)}) copy-start(bf16[512,768]{1,0:T(8,128)(2,1)S(1)} %fusion.49) | copy-start | bytes 2359300
  167.2 9.6 %collective-permute-start.6 = (bf16[512,768]{1,0:T(8,128)(2,1)S(1)}, bf16[512,768]{1,0:T(8,128)(2,1)S(1)}, u32[]{:S(2)}, u32[]{:S(2)}) collective-permute-start(bf16[512,768]{1,0:T(8,128)(2,1)S(1)} %fusion.49), channel_id=1, source_target_pairs={{0,1},{1,0},{2,3},{3,2},{4,5},{5,4},{6,7},{7,6},{8,9},{9,8},{10,11... | collective-permute-start | bytes 2359304 | tf_op jit(solution)/shard_map/ppermute | solution.py:150
  167.8 8.7 %copy-start.9 = (bf16[512,768]{1,0:T(8,128)(2,1)}, bf16[512,768]{1,0:T(8,128)(2,1)S(1)}, u32[]{:S(2)}) copy-start(bf16[512,768]{1,0:T(8,128)(2,1)S(1)} %fusion.48) | copy-start | bytes 2359300
  167.8 9.0 %collective-permute-start.10 = (bf16[512,768]{1,0:T(8,128)(2,1)S(1)}, bf16[512,768]{1,0:T(8,128)(2,1)S(1)}, u32[]{:S(2)}, u32[]{:S(2)}) collective-permute-start(bf16[512,768]{1,0:T(8,128)(2,1)S(1)} %fusion.48), channel_id=1, source_target_pairs={{0,1},{1,0},{2,3},{3,2},{4,5},{5,4},{6,7},{7,6},{8,9},{9,8},{10,11... | collective-permute-start | bytes 2359304 | tf_op jit(solution)/shard_map/ppermute | solution.py:150
  188.6 88.9 %copy-start.13 = (s32[96]{0:T(128)S(1)}, s32[96]{0:T(128)}, u32[]{:S(2)}) copy-start(s32[96]{0:T(128)} %param.10) | copy-start | bytes 1156
  188.7 171.0 %all-gather.5.cloned.1.call-start = ((), (), s32[]{:S(2)}) async-start(), calls=%async_computation.4 | async-start | bytes 4718592 | tf_op jit(solution)/shard_map/all_gather | solution.py:159
  188.7 24.8 %collective-permute-start.11 = (bf16[320,1536]{1,0:T(8,128)(2,1)S(1)}, bf16[320,1536]{1,0:T(8,128)(2,1)S(1)}, u32[]{:S(2)}, u32[]{:S(2)}) collective-permute-start(bf16[320,1536]{1,0:T(8,128)(2,1)S(1)} %get-tuple-element.24), channel_id=1, source_target_pairs={{0,16},{16,0},{1,17},{17,1},{2,18},{18,2},{3,19},{19,3},{4,20},{20... | collective-permute-start | bytes 2949128 | tf_op jit(solution)/shard_map/ppermute | solution.py:22
  190.3 33.8 %collective-permute-start.13 = (bf16[160,1536]{1,0:T(8,128)(2,1)S(1)}, bf16[160,1536]{1,0:T(8,128)(2,1)S(1)}, u32[]{:S(2)}, u32[]{:S(2)}) collective-permute-start(bf16[160,1536]{1,0:T(8,128)(2,1)S(1)} %get-tuple-element.20), channel_id=1, source_target_pairs={{0,16},{16,0},{1,17},{17,1},{2,18},{18,2},{3,19},{19,3},{4,20},{20... | collective-permute-start | bytes 1474568 | tf_op jit(solution)/shard_map/ppermute | solution.py:22
  190.8 41.6 %collective-permute-start.12 = (bf16[160,1536]{1,0:T(8,128)(2,1)S(1)}, bf16[160,1536]{1,0:T(8,128)(2,1)}, u32[]{:S(2)}, u32[]{:S(2)}) collective-permute-start(bf16[160,1536]{1,0:T(8,128)(2,1)S(1)} %get-tuple-element.22), channel_id=1, source_target_pairs={{0,16},{16,0},{1,17},{17,1},{2,18},{18,2},{3,19},{19,3},{4,20},{20... | collective-permute-start | bytes 1474568 | tf_op jit(solution)/shard_map/ppermute | solution.py:22
  213.5 10.5 %copy-start.5 = (bf16[320,1536]{1,0:T(8,128)(2,1)}, bf16[320,1536]{1,0:T(8,128)(2,1)S(1)}, u32[]{:S(2)}) copy-start(bf16[320,1536]{1,0:T(8,128)(2,1)S(1)} %collective-permute-done.11) | copy-start | bytes 2949124
  224.0 52.2 %copy-start.11 = (bf16[160,1536]{1,0:T(8,128)(2,1)}, bf16[160,1536]{1,0:T(8,128)(2,1)S(1)}, u32[]{:S(2)}) copy-start(bf16[160,1536]{1,0:T(8,128)(2,1)S(1)} %collective-permute-done.13) | copy-start | bytes 1474564
  275.0 9.0 %copy-start = (bf16[128,2048]{1,0:T(8,128)(2,1)S(1)}, bf16[128,2048]{1,0:T(8,128)(2,1)}, u32[]{:S(2)}) copy-start(bf16[128,2048]{1,0:T(8,128)(2,1)} %reduce-scatter.2.cloned.1.call-done) | copy-start | bytes 1572868
  362.4 29.3 %collective-permute-start.15 = (bf16[512,2048]{1,0:T(8,128)(2,1)S(1)}, bf16[512,2048]{1,0:T(8,128)(2,1)S(1)}, u32[]{:S(2)}, u32[]{:S(2)}) collective-permute-start(bf16[512,2048]{1,0:T(8,128)(2,1)S(1)} %get-tuple-element.30), channel_id=1, source_target_pairs={{0,1},{1,0},{2,3},{3,2},{4,5},{5,4},{6,7},{7,6},{8,9},{9,8},{10,11... | collective-permute-start | bytes 6291464 | tf_op jit(solution)/shard_map/ppermute | solution.py:150
  368.0 22.6 %collective-permute-start.14 = (bf16[640,768]{1,0:T(8,128)(2,1)S(1)}, bf16[640,768]{1,0:T(8,128)(2,1)S(1)}, u32[]{:S(2)}, u32[]{:S(2)}) collective-permute-start(bf16[640,768]{1,0:T(8,128)(2,1)S(1)} %bitcast.84), channel_id=1, source_target_pairs={{0,16},{16,0},{1,17},{17,1},{2,18},{18,2},{3,19},{19,3},{4,20},{20... | collective-permute-start | bytes 2949128 | tf_op jit(solution)/shard_map/ppermute | solution.py:22
  369.5 25.9 %collective-permute-start.17 = (bf16[512,2048]{1,0:T(8,128)(2,1)S(1)}, bf16[512,2048]{1,0:T(8,128)(2,1)S(1)}, u32[]{:S(2)}, u32[]{:S(2)}) collective-permute-start(bf16[512,2048]{1,0:T(8,128)(2,1)S(1)} %get-tuple-element.31), channel_id=1, source_target_pairs={{0,1},{1,0},{2,3},{3,2},{4,5},{5,4},{6,7},{7,6},{8,9},{9,8},{10,11... | collective-permute-start | bytes 6291464 | tf_op jit(solution)/shard_map/ppermute | solution.py:150
  393.9 14.3 %collective-permute-start.16 = (bf16[320,768]{1,0:T(8,128)(2,1)S(1)}, bf16[320,768]{1,0:T(8,128)(2,1)S(1)}, u32[]{:S(2)}, u32[]{:S(2)}) collective-permute-start(bf16[320,768]{1,0:T(8,128)(2,1)S(1)} %bitcast.86), channel_id=1, source_target_pairs={{0,16},{16,0},{1,17},{17,1},{2,18},{18,2},{3,19},{19,3},{4,20},{20... | collective-permute-start | bytes 1474568 | tf_op jit(solution)/shard_map/ppermute | solution.py:22
  397.6 18.0 %collective-permute-start.18 = (bf16[320,768]{1,0:T(8,128)(2,1)S(1)}, bf16[320,768]{1,0:T(8,128)(2,1)S(1)}, u32[]{:S(2)}, u32[]{:S(2)}) collective-permute-start(bf16[320,768]{1,0:T(8,128)(2,1)S(1)} %bitcast.87), channel_id=1, source_target_pairs={{0,16},{16,0},{1,17},{17,1},{2,18},{18,2},{3,19},{19,3},{4,20},{20... | collective-permute-start | bytes 1474568 | tf_op jit(solution)/shard_map/ppermute | solution.py:22
  408.2 8.0 %copy-start.27 = (bf16[4,80,2048]{2,1,0:T(8,128)(2,1)S(1)}, bf16[4,80,2048]{2,1,0:T(8,128)(2,1)}, u32[]{:S(2)}) copy-start(bf16[4,80,2048]{2,1,0:T(8,128)(2,1)} %copy-done.26) | copy-start | bytes 3932164
  (19 other events, 77.0 us)
Sparse Core Ops, SparseCore 0:
  10.1 76.2 all-gather.2
  188.8 86.2 reduce-scatter.1
  286.5 73.1 all-gather.4

commit v4 on v3

--- a/solution.py
+++ b/solution.py
@@ -6,6 +6,7 @@
 D = 4096
 TOP = 8
 EPSILON = 1e-06
+GROUPS = 4
 BF = jnp.bfloat16
 F32 = jnp.float32
 
@@ -155,13 +156,11 @@
     return [list(range(core, count, 2)) for core in range(2)]
 
 
-def gather_core(value):
-    return lax.all_gather(value, "ep", axis=0, tiled=True, axis_index_groups=same_core())
-
-
-def with_other_core(mine):
-    half = mine.shape[0] // 2
-    return [mine, across(mine[:half]), across(mine[half:])]
+def of_core(value, core, rows):
+    count = value.shape[0] // rows
+    value = value.reshape(count // 2, 2, rows, value.shape[1])
+    picked = lax.dynamic_index_in_dim(value, core, 1, keepdims=False)
+    return picked.reshape(count // 2 * rows, value.shape[3])
 
 
 def local(signal, routes, gates, pairing, w_gate, w_up, w_down):
@@ -172,25 +171,21 @@
     capacity = min(row_count, row_count * TOP * 5 // (4 * experts))
     w_gate, w_up, w_down = w_gate[0], w_up[0], w_down[0]
     hidden_width = w_gate.shape[1]
-    half, quarter = experts // 2, experts // 4
-    spans = ((0, half), (half, half + quarter), (half + quarter, experts))
-
-    mine, w_down_other = lax.optimization_barrier((gather_core(signal), across(w_down)))
-    row_groups = with_other_core(mine)
+    group = experts // GROUPS
+    spans = [(low, low + group) for low in range(0, experts, group)]
+
+    rows_all = lax.all_gather(signal, "ep", axis=0, tiled=True)
+    rows_all, w_down_other = lax.optimization_barrier((rows_all, across(w_down)))
     w_down_pair = jnp.concatenate([w_down, w_down_other], 0)
     w_both = jnp.concatenate([w_gate, w_up], 1)
-    weight = gate_table(routes, gates, experts).reshape(half, 2, row_count)
-    weight = jnp.where(
-        core == 0,
-        jnp.concatenate([weight[:, 0], weight[:, 1]], 0),
-        jnp.concatenate([weight[:, 1], weight[:, 0]], 0),
-    )
+    weight = gate_table(routes, gates, experts)
     pick = slot_picks(weight, capacity)
     row_weight = weight.reshape(experts * row_count, 1)
 
-    arrived, gate_up, weighted, handed = [], [], [], []
-    for (low, high), rows in zip(spans, row_groups):
+    arrived, gate_up, weighted, kept, handed = [], [], [], [], []
+    for low, high in spans:
         count = high - low
+        rows = rows_all[low * row_count : high * row_count]
         chosen = pick[low:high]
         arrived.append(
             blocks_mm(chosen, rows.reshape(count, row_count, width), 2, 1)
@@ -206,10 +201,10 @@
             count * row_count, hidden_width
         )
         weighted.append((spread * row_weight[low * row_count : high * row_count]).astype(BF))
-        if low > 0:
-            handed.append(across(weighted[-1]))
-
-    inner = jnp.concatenate([weighted[0], jnp.concatenate(handed, 0)], 1)
+        kept.append(of_core(weighted[-1], core, row_count))
+        handed.append(across(of_core(weighted[-1], 1 - core, row_count)))
+
+    inner = jnp.concatenate([jnp.concatenate(kept, 0), jnp.concatenate(handed, 0)], 1)
     returned = mm(inner, w_down_pair).astype(BF)
     combined = lax.psum_scatter(
         returned, "ep", scatter_dimension=0, tiled=True, axis_index_groups=same_core()
@@ -219,10 +214,11 @@
     mixed = combined
     grad_rows = row_gradient(combined.astype(F32), pairing)
 
-    grad_groups = with_other_core(gather_core(grad_rows))
+    grads_all = lax.all_gather(grad_rows, "ep", axis=0, tiled=True)
     gate_pre, up_pre = [], []
-    for (low, high), rows, own, other in zip(spans, grad_groups, gate_up, others):
+    for (low, high), own, other in zip(spans, gate_up, others):
         count = high - low
+        rows = grads_all[low * row_count : high * row_count]
         product = (mm(rows, w_down, 1, 1) * row_weight[low * row_count : high * row_count]).astype(BF)
         sent = (
             blocks_mm(pick[low:high], product.reshape(count, row_count, hidden_width), 2, 1)
@@ -237,9 +233,7 @@
             (grad_hidden * up * sigma * (1.0 + gate * (1.0 - sigma))).astype(BF)
         )
         up_pre.append((grad_hidden * gate * sigma).astype(BF))
-    grad_down = mm(
-        jnp.concatenate(weighted, 0), jnp.concatenate(grad_groups, 0), 0, 0
-    ).astype(BF)
+    grad_down = mm(jnp.concatenate(weighted, 0), grads_all, 0, 0).astype(BF)
     arrived = jnp.concatenate(arrived, 0)
     grad_gate = mm(arrived, jnp.concatenate(gate_pre, 0), 0, 0).astype(BF)
     grad_up = mm(arrived, jnp.concatenate(up_pre, 0), 0, 0).astype(BF)

time: 441 us -> 429 us (0.973)
  waiting for transfers between devices: 305 us -> 278 us
  other arithmetic: 13.8 us -> 27.9 us
  local copies, waits for them, and re-layouts: 15.8 us -> 7.95 us
  starting transfers between devices: 23.2 us -> 28.2 us
    ppermute x12 -> x16, waiting for transfers between devices: 119 us -> 102 us  [swap(): return lax.ppermute(value, 'rep', [(0, 1), (1, 0)])]
    all_gather x2, waiting for transfers between devices: 136 us -> 127 us  [the longest x1 64.6 us: local(): rows_all = lax.all_gather(signal, 'ep', axis=0, tiled=True)]
    convert_element_type x3 -> x4, other arithmetic: 2.29 us -> 9.99 us  [local(): both = both_halves(own, other, rank).astype(F32)]
    ppermute x12 -> x16, starting transfers between devices: 14.6 us -> 19.4 us  [swap(): return lax.ppermute(value, 'rep', [(0, 1), (1, 0)])]
    dot_general x10 -> x12, matrix products: 50 us -> 52.9 us  [mm(): lax.dot_general(a, b, (((ca,), (cb,)), ((), ())), preferred_element_type=...]
  transfers between devices with their start and end apart: 23 -> 25, of which waited for: 15 -> 19; matrix products, arithmetic and copies ran while one was open for 10% -> 12% of each run, Pallas kernels for 0% -> 0%
where the time goes in v4:
time: 429 us; the launch traced here: 423 us
  waiting for transfers between devices  278 us (65%)
  matrix products  60.4 us (14%)
  starting transfers between devices  28.2 us (7%)
  other arithmetic  27.9 us (7%)
  between operations  14.9 us (3%)
  local copies, waits for them, and re-layouts  7.95 us (2%)
  blocking collectives  5.15 us (1%)
    ppermute x16, waiting for transfers between devices, swap(): return lax.ppermute(value, 'rep', [(0, 1), (1, 0)])  102 us
    all_gather x1, waiting for transfers between devices, local(): rows_all = lax.all_gather(signal, 'ep', axis=0, tiled=True)  64.6 us
    all_gather x1, waiting for transfers between devices, local(): grads_all = lax.all_gather(grad_rows, 'ep', axis=0, tiled=True)  62.1 us
    dot_general x12, matrix products, mm(): lax.dot_general(a, b, (((ca,), (cb,)), ((), ())), preferred_element_type=...  52.9 us
    reduce_scatter x1, waiting for transfers between devices, local(): lax.psum_scatter(returned, 'ep', scatter_dimension=0, tiled=True, axis_in...  41.2 us
    ppermute x16, starting transfers between devices, swap(): return lax.ppermute(value, 'rep', [(0, 1), (1, 0)])  19.4 us
    convert_element_type x4, other arithmetic, local(): both = both_halves(own, other, rank).astype(F32)  9.99 us
  transfers between devices with their start and end apart: 25, of which 19 were waited for; matrix products, arithmetic and copies ran while one was open for 12% of the time, Pallas kernels for 0%

profile of v4, /device:TPU:0, one launch (start us, length us, event | category | flops | bytes accessed | tf_op | source)
XLA Modules:
  0.0 422.5 jit_solution(10627448166006681504)
XLA Ops:
  9.7 7.0 %all-to-all-start = ((f32[16,1,128]{2,1,0:T(1,128)}), f32[16,1,128]{2,1,0:T(1,128)S(1)}, u32[]{:S(2)}, u32[]{:S(2)}) async-start(f32[16,1,128]{2,1,0:T(1,128)} %bitcast.2), calls=%async_computation | async-start | bytes 16384 | tf_op jit(solution)/shard_map/all_to_all | solution.py:82
  16.8 6.3 %all-to-all-done = f32[16,1,128]{2,1,0:T(1,128)S(1)} async-done(((f32[16,1,128]{2,1,0:T(1,128)}), f32[16,1,128]{2,1,0:T(1,128)S(1)}, u32[]{:S(2)}, u32[]{:S(2)}) %all-to-all-start) | async-done | bytes 8224 | tf_op jit(solution)/shard_map/all_to_all | solution.py:82
  23.3 64.6 %all-gather.3.cloned.1.call-done = bf16[2048,2048]{1,0:T(8,128)(2,1)} async-done(((bf16[128,2048]{1,0:T(8,128)(2,1)}), bf16[2048,2048]{1,0:T(8,128)(2,1)}) %all-gather.3.cloned.1.call-update) | async-done | bytes 8388624 | tf_op jit(solution)/shard_map/all_gather | solution.py:177
  87.9 3.9 fusion.149
  94.2 3.2 convolution_convert_fusion.10
  99.6 3.2 convolution_convert_fusion.9
  104.0 3.2 convolution_convert_fusion.7
  109.4 3.4 convolution_convert_fusion.8
  116.1 6.1 %collective-permute-done.3 = bf16[160,1536]{1,0:T(8,128)(2,1)S(1)} collective-permute-done((bf16[160,1536]{1,0:T(8,128)(2,1)S(1)}, bf16[160,1536]{1,0:T(8,128)(2,1)S(1)}, u32[]{:S(2)}, u32[]{:S(2)}) %collective-permute-start.3) | collective-permute-done | bytes 491552 | tf_op jit(solution)/shard_map/ppermute | solution.py:23
  124.8 7.9 %collective-permute-done.7 = bf16[160,1536]{1,0:T(8,128)(2,1)S(1)} collective-permute-done((bf16[160,1536]{1,0:T(8,128)(2,1)S(1)}, bf16[160,1536]{1,0:T(8,128)(2,1)S(1)}, u32[]{:S(2)}, u32[]{:S(2)}) %collective-permute-start.7) | collective-permute-done | bytes 491552 | tf_op jit(solution)/shard_map/ppermute | solution.py:23
  135.3 7.9 %collective-permute-done.5 = bf16[160,1536]{1,0:T(8,128)(2,1)S(1)} collective-permute-done((bf16[160,1536]{1,0:T(8,128)(2,1)S(1)}, bf16[160,1536]{1,0:T(8,128)(2,1)S(1)}, u32[]{:S(2)}, u32[]{:S(2)}) %collective-permute-start.5) | collective-permute-done | bytes 491552 | tf_op jit(solution)/shard_map/ppermute | solution.py:23
  148.5 5.3 %collective-permute-done.4 = bf16[160,768]{1,0:T(8,128)(2,1)S(1)} collective-permute-done((bf16[160,768]{1,0:T(8,128)(2,1)S(1)}, bf16[160,768]{1,0:T(8,128)(2,1)S(1)}, u32[]{:S(2)}, u32[]{:S(2)}) %collective-permute-start.4) | collective-permute-done | bytes 245792 | tf_op jit(solution)/shard_map/ppermute | solution.py:23
  156.0 3.0 collective-permute-done.8
  159.0 4.6 %collective-permute-done.6 = bf16[160,768]{1,0:T(8,128)(2,1)S(1)} collective-permute-done((bf16[160,768]{1,0:T(8,128)(2,1)S(1)}, bf16[160,768]{1,0:T(8,128)(2,1)S(1)}, u32[]{:S(2)}, u32[]{:S(2)}) %collective-permute-start.6) | collective-permute-done | bytes 245792 | tf_op jit(solution)/shard_map/ppermute | solution.py:23
  168.4 8.7 %fusion.4 = bf16[1024,2048]{1,0:T(8,128)(2,1)} fusion(bf16[768,2048]{1,0:T(8,128)(2,1)S(1)} %copy-done.26, bf16[768,2048]{1,0:T(8,128)(2,1)S(1)} %bitcast.154, bf16[256,768]{1,0:T(8,128)(2,1)S(1)} %collective-permute-done.12, bf16[256,768]{1,0:T(8,128)(2,1)S(1)} %collective-permute-done.11, bf16[256,768]{1,0:T(8,128)(2,1)S(1)} %collective-permute-done.10, ...), kind=kOutput, calls=%fused_computation.6 | convolution fusion | flops 6482296832 | bytes 13631488 | tf_op jit(solution)/shard_map/dot_general | solution.py:15
  181.2 10.3 %collective-permute-done.13 = bf16[160,1536]{1,0:T(8,128)(2,1)} collective-permute-done((bf16[160,1536]{1,0:T(8,128)(2,1)}, bf16[160,1536]{1,0:T(8,128)(2,1)}, u32[]{:S(2)}, u32[]{:S(2)}) %collective-permute-start.13) | collective-permute-done | bytes 491552 | tf_op jit(solution)/shard_map/ppermute | solution.py:23
  191.6 10.5 %collective-permute-done.14 = bf16[160,1536]{1,0:T(8,128)(2,1)} collective-permute-done((bf16[160,1536]{1,0:T(8,128)(2,1)}, bf16[160,1536]{1,0:T(8,128)(2,1)}, u32[]{:S(2)}, u32[]{:S(2)}) %collective-permute-start.14) | collective-permute-done | bytes 491552 | tf_op jit(solution)/shard_map/ppermute | solution.py:23
  202.1 10.5 %collective-permute-done.16 = bf16[160,1536]{1,0:T(8,128)(2,1)} collective-permute-done((bf16[160,1536]{1,0:T(8,128)(2,1)}, bf16[160,1536]{1,0:T(8,128)(2,1)}, u32[]{:S(2)}, u32[]{:S(2)}) %collective-permute-start.16) | collective-permute-done | bytes 491552 | tf_op jit(solution)/shard_map/ppermute | solution.py:23
  212.6 9.7 %collective-permute-done.15 = bf16[160,1536]{1,0:T(8,128)(2,1)} collective-permute-done((bf16[160,1536]{1,0:T(8,128)(2,1)}, bf16[160,1536]{1,0:T(8,128)(2,1)}, u32[]{:S(2)}, u32[]{:S(2)}) %collective-permute-start.15) | collective-permute-done | bytes 491552 | tf_op jit(solution)/shard_map/ppermute | solution.py:23
  222.4 41.2 %reduce-scatter.2.cloned.1.call-done = bf16[128,2048]{1,0:T(8,128)(2,1)} async-done(((bf16[1024,2048]{1,0:T(8,128)(2,1)}), bf16[128,2048]{1,0:T(8,128)(2,1)}) %reduce-scatter.2.cloned.1.call-update) | async-done | bytes 524304 | tf_op jit(solution)/shard_map/reduce_scatter | solution.py:209
  268.1 5.2 %psum.7 = f32[224]{0:T(256)S(1)} all-reduce(f32[224]{0:T(256)S(1)} %pad_maximum_fusion.4), channel_id=1, replica_groups=mesh['rep'=2,'ep'=16] {'rep'}, use_global_device_ids=true, to_apply=%region_4.5 | all-reduce | flops 224 | bytes 1792 | tf_op jit(solution)/shard_map/psum | solution.py:51
  280.6 2.8 fusion.83
  283.4 2.8 fusion.84
  286.2 2.9 fusion.85
  290.6 62.1 %all-gather.5.cloned.1.call-done = bf16[2048,2048]{1,0:T(8,128)(2,1)} async-done(((bf16[128,2048]{1,0:T(8,128)(2,1)}), bf16[2048,2048]{1,0:T(8,128)(2,1)}) %all-gather.5.cloned.1.call-update) | async-done | bytes 8388624 | tf_op jit(solution)/shard_map/all_gather | solution.py:217
  352.7 4.5 %multiply_convert_fusion.3 = bf16[512,768]{1,0:T(8,128)(2,1)S(1)} fusion(bf16[2048,2048]{1,0:T(8,128)(2,1)} %all-gather.5.cloned.1.call-done, f32[512]{0:T(512)} %bitcast.144, bf16[1,768,2048]{2,1,0:T(8,128)(2,1)} %param.13), kind=kOutput, calls=%fused_computation.77 | convolution fusion | flops 1611399168 | bytes 6031360 | tf_op jit(solution)/shard_map/dot_general | solution.py:15
  368.7 8.7 %fusion.29 = bf16[1,768,2048]{2,1,0:T(8,128)(2,1)} fusion(bf16[2048,2048]{1,0:T(8,128)(2,1)S(1)} %copy-done.20, bf16[512,768]{1,0:T(8,128)(2,1)S(1)} %fusion.56, bf16[512,768]{1,0:T(8,128)(2,1)S(1)} %fusion.57, bf16[512,768]{1,0:T(8,128)(2,1)S(1)} %copy-done.13, bf16[512,768]{1,0:T(8,128)(2,1)S(1)} %copy-done.12), kind=kOutput, calls=%fused_computation.32 | convolution fusion | flops 6456606720 | bytes 14680064 | tf_op jit(solution)/shard_map/dot_general | solution.py:15
  378.0 4.2 collective-permute-done.18
  382.8 9.9 %collective-permute-done.19 = bf16[320,768]{1,0:T(8,128)(2,1)S(1)} collective-permute-done((bf16[320,768]{1,0:T(8,128)(2,1)S(1)}, bf16[320,768]{1,0:T(8,128)(2,1)S(1)}, u32[]{:S(2)}, u32[]{:S(2)}) %collective-permute-start.19) | collective-permute-done | bytes 491552 | tf_op jit(solution)/shard_map/ppermute | solution.py:23
  393.3 9.3 %collective-permute-done.20 = bf16[320,768]{1,0:T(8,128)(2,1)S(1)} collective-permute-done((bf16[320,768]{1,0:T(8,128)(2,1)S(1)}, bf16[320,768]{1,0:T(8,128)(2,1)S(1)}, u32[]{:S(2)}, u32[]{:S(2)}) %collective-permute-start.20) | collective-permute-done | bytes 491552 | tf_op jit(solution)/shard_map/ppermute | solution.py:23
  403.1 6.2 %fusion.33 = bf16[1,2048,768]{2,1,0:T(8,128)(2,1)} fusion(bf16[320,768]{1,0:T(8,128)(2,1)S(1)} %get-tuple-element.40, bf16[320,768]{1,0:T(8,128)(2,1)S(1)} %get-tuple-element.38, bf16[320,768]{1,0:T(8,128)(2,1)S(1)} %get-tuple-element.36, bf16[320,768]{1,0:T(8,128)(2,1)S(1)} %get-tuple-element.34, bf16[320,2048]{1,0:T(8,128)(2,1)S(1)} %bitcast.162, ...), kind=kOutput, calls=%fused_computation.34 | convolution fusion | flops 4056940544 | bytes 10354688 | tf_op jit(solution)/shard_map/dot_general | solution.py:15
  409.4 6.2 %fusion.32 = bf16[1,2048,768]{2,1,0:T(8,128)(2,1)} fusion(bf16[320,768]{1,0:T(8,128)(2,1)S(1)} %get-tuple-element.41, bf16[320,768]{1,0:T(8,128)(2,1)S(1)} %get-tuple-element.39, bf16[320,768]{1,0:T(8,128)(2,1)S(1)} %get-tuple-element.37, bf16[320,768]{1,0:T(8,128)(2,1)S(1)} %get-tuple-element.35, bf16[320,2048]{1,0:T(8,128)(2,1)S(1)} %bitcast.163, ...), kind=kOutput, calls=%fused_computation.33 | convolution fusion | flops 4056940544 | bytes 10354688 | tf_op jit(solution)/shard_map/dot_general | solution.py:15
  (171 shorter events, 62.5 us)
Async XLA Ops:
  7.2 80.7 %all-gather.3.cloned.1.call-start = ((), (), s32[]{:S(2)}) async-start(), calls=%async_computation.2 | async-start | bytes 8912896 | tf_op jit(solution)/shard_map/all_gather | solution.py:177
  7.9 15.4 %collective-permute-start = (bf16[768,2048]{1,0:T(8,128)(2,1)}, bf16[768,2048]{1,0:T(8,128)(2,1)S(1)}, u32[]{:S(2)}, u32[]{:S(2)}) collective-permute-start(bf16[768,2048]{1,0:T(8,128)(2,1)} %bitcast.153), channel_id=1, source_target_pairs={{0,1},{1,0},{2,3},{3,2},{4,5},{5,4},{6,7},{7,6},{8,9},{9,8},{10,11... | collective-permute-start | bytes 9437192 | tf_op jit(solution)/shard_map/ppermute | solution.py:151
  9.7 13.4 %all-to-all-start = ((f32[16,1,128]{2,1,0:T(1,128)}), f32[16,1,128]{2,1,0:T(1,128)S(1)}, u32[]{:S(2)}, u32[]{:S(2)}) async-start(f32[16,1,128]{2,1,0:T(1,128)} %bitcast.2), calls=%async_computation | async-start | bytes 16384 | tf_op jit(solution)/shard_map/all_to_all | solution.py:82
  16.8 246.8 %reduce-scatter.2.cloned.1.call-start = ((), (), s32[]{:S(2)}) async-start(), calls=%async_computation.3 | async-start | bytes 4718592 | tf_op jit(solution)/shard_map/reduce_scatter | solution.py:209
  23.2 254.6 %copy-start.18 = (f32[4,1,128]{2,1,0:T(1,128)}, f32[4,1,128]{2,1,0:T(1,128)S(1)}, u32[]{:S(2)}) copy-start(f32[4,1,128]{2,1,0:T(1,128)S(1)} %get-tuple-element.50) | copy-start | bytes 6148
  23.2 255.7 %copy-start.16 = (f32[4,1,128]{2,1,0:T(1,128)}, f32[4,1,128]{2,1,0:T(1,128)S(1)}, u32[]{:S(2)}) copy-start(f32[4,1,128]{2,1,0:T(1,128)S(1)} %get-tuple-element.53) | copy-start | bytes 6148
  23.3 256.7 %copy-start.14 = (f32[4,1,128]{2,1,0:T(1,128)}, f32[4,1,128]{2,1,0:T(1,128)S(1)}, u32[]{:S(2)}) copy-start(f32[4,1,128]{2,1,0:T(1,128)S(1)} %get-tuple-element.52) | copy-start | bytes 6148
  23.3 68.5 %copy-start.25 = (bf16[768,2048]{1,0:T(8,128)(2,1)}, bf16[768,2048]{1,0:T(8,128)(2,1)S(1)}, u32[]{:S(2)}) copy-start(bf16[768,2048]{1,0:T(8,128)(2,1)S(1)} %collective-permute-done) | copy-start | bytes 9437188
  97.5 15.9 %collective-permute-start.1 = (bf16[160,1536]{1,0:T(8,128)(2,1)S(1)}, bf16[160,1536]{1,0:T(8,128)(2,1)S(1)}, u32[]{:S(2)}, u32[]{:S(2)}) collective-permute-start(bf16[160,1536]{1,0:T(8,128)(2,1)S(1)} %constant_dynamic-slice_fusion.11), channel_id=1, source_target_pairs={{0,16},{16,0},{1,17},{17,1},{2,18},{18,2},{3,19},{19,3},{4,20},{20... | collective-permute-start | bytes 1474568 | tf_op jit(solution)/shard_map/ppermute | solution.py:23
  102.9 19.3 %collective-permute-start.3 = (bf16[160,1536]{1,0:T(8,128)(2,1)S(1)}, bf16[160,1536]{1,0:T(8,128)(2,1)S(1)}, u32[]{:S(2)}, u32[]{:S(2)}) collective-permute-start(bf16[160,1536]{1,0:T(8,128)(2,1)S(1)} %constant_dynamic-slice_fusion.9), channel_id=1, source_target_pairs={{0,16},{16,0},{1,17},{17,1},{2,18},{18,2},{3,19},{19,3},{4,20},{20... | collective-permute-start | bytes 1474568 | tf_op jit(solution)/shard_map/ppermute | solution.py:23
  107.3 25.4 %collective-permute-start.7 = (bf16[160,1536]{1,0:T(8,128)(2,1)S(1)}, bf16[160,1536]{1,0:T(8,128)(2,1)S(1)}, u32[]{:S(2)}, u32[]{:S(2)}) collective-permute-start(bf16[160,1536]{1,0:T(8,128)(2,1)S(1)} %constant_dynamic-slice_fusion.5), channel_id=1, source_target_pairs={{0,16},{16,0},{1,17},{17,1},{2,18},{18,2},{3,19},{19,3},{4,20},{20... | collective-permute-start | bytes 1474568 | tf_op jit(solution)/shard_map/ppermute | solution.py:23
  112.8 30.4 %collective-permute-start.5 = (bf16[160,1536]{1,0:T(8,128)(2,1)S(1)}, bf16[160,1536]{1,0:T(8,128)(2,1)S(1)}, u32[]{:S(2)}, u32[]{:S(2)}) collective-permute-start(bf16[160,1536]{1,0:T(8,128)(2,1)S(1)} %constant_dynamic-slice_fusion.7), channel_id=1, source_target_pairs={{0,16},{16,0},{1,17},{17,1},{2,18},{18,2},{3,19},{19,3},{4,20},{20... | collective-permute-start | bytes 1474568 | tf_op jit(solution)/shard_map/ppermute | solution.py:23
  114.5 34.0 %collective-permute-start.2 = (bf16[160,768]{1,0:T(8,128)(2,1)S(1)}, bf16[160,768]{1,0:T(8,128)(2,1)S(1)}, u32[]{:S(2)}, u32[]{:S(2)}) collective-permute-start(bf16[160,768]{1,0:T(8,128)(2,1)S(1)} %fusion.108), channel_id=1, source_target_pairs={{0,16},{16,0},{1,17},{17,1},{2,18},{18,2},{3,19},{19,3},{4,20},{20... | collective-permute-start | bytes 737288 | tf_op jit(solution)/shard_map/ppermute | solution.py:23
  123.2 30.5 %collective-permute-start.4 = (bf16[160,768]{1,0:T(8,128)(2,1)S(1)}, bf16[160,768]{1,0:T(8,128)(2,1)S(1)}, u32[]{:S(2)}, u32[]{:S(2)}) collective-permute-start(bf16[160,768]{1,0:T(8,128)(2,1)S(1)} %fusion.107), channel_id=1, source_target_pairs={{0,16},{16,0},{1,17},{17,1},{2,18},{18,2},{3,19},{19,3},{4,20},{20... | collective-permute-start | bytes 737288 | tf_op jit(solution)/shard_map/ppermute | solution.py:23
  133.8 25.2 %collective-permute-start.8 = (bf16[160,768]{1,0:T(8,128)(2,1)S(1)}, bf16[160,768]{1,0:T(8,128)(2,1)S(1)}, u32[]{:S(2)}, u32[]{:S(2)}) collective-permute-start(bf16[160,768]{1,0:T(8,128)(2,1)S(1)} %fusion.105), channel_id=1, source_target_pairs={{0,16},{16,0},{1,17},{17,1},{2,18},{18,2},{3,19},{19,3},{4,20},{20... | collective-permute-start | bytes 737288 | tf_op jit(solution)/shard_map/ppermute | solution.py:23
  144.3 19.3 %collective-permute-start.6 = (bf16[160,768]{1,0:T(8,128)(2,1)S(1)}, bf16[160,768]{1,0:T(8,128)(2,1)S(1)}, u32[]{:S(2)}, u32[]{:S(2)}) collective-permute-start(bf16[160,768]{1,0:T(8,128)(2,1)S(1)} %fusion.106), channel_id=1, source_target_pairs={{0,16},{16,0},{1,17},{17,1},{2,18},{18,2},{3,19},{19,3},{4,20},{20... | collective-permute-start | bytes 737288 | tf_op jit(solution)/shard_map/ppermute | solution.py:23
  154.7 12.1 %collective-permute-start.9 = (bf16[256,768]{1,0:T(8,128)(2,1)S(1)}, bf16[256,768]{1,0:T(8,128)(2,1)S(1)}, u32[]{:S(2)}, u32[]{:S(2)}) collective-permute-start(bf16[256,768]{1,0:T(8,128)(2,1)S(1)} %bitcast.126), channel_id=1, source_target_pairs={{0,1},{1,0},{2,3},{3,2},{4,5},{5,4},{6,7},{7,6},{8,9},{9,8},{10,11... | collective-permute-start | bytes 1179656 | tf_op jit(solution)/shard_map/ppermute | solution.py:151
  155.5 11.4 %collective-permute-start.10 = (bf16[256,768]{1,0:T(8,128)(2,1)S(1)}, bf16[256,768]{1,0:T(8,128)(2,1)S(1)}, u32[]{:S(2)}, u32[]{:S(2)}) collective-permute-start(bf16[256,768]{1,0:T(8,128)(2,1)S(1)} %bitcast.127), channel_id=1, source_target_pairs={{0,1},{1,0},{2,3},{3,2},{4,5},{5,4},{6,7},{7,6},{8,9},{9,8},{10,11... | collective-permute-start | bytes 1179656 | tf_op jit(solution)/shard_map/ppermute | solution.py:151
  164.7 2.2 collective-permute-start.11
  166.3 1.8 collective-permute-start.12
  177.0 88.9 %copy-start.19 = (s32[96]{0:T(128)S(1)}, s32[96]{0:T(128)}, u32[]{:S(2)}) copy-start(s32[96]{0:T(128)} %param.10) | copy-start | bytes 1156
  177.1 175.6 %all-gather.5.cloned.1.call-start = ((), (), s32[]{:S(2)}) async-start(), calls=%async_computation.4 | async-start | bytes 8912896 | tf_op jit(solution)/shard_map/all_gather | solution.py:217
  177.1 14.4 %collective-permute-start.13 = (bf16[160,1536]{1,0:T(8,128)(2,1)}, bf16[160,1536]{1,0:T(8,128)(2,1)}, u32[]{:S(2)}, u32[]{:S(2)}) collective-permute-start(bf16[160,1536]{1,0:T(8,128)(2,1)} %get-tuple-element.28), channel_id=1, source_target_pairs={{0,16},{16,0},{1,17},{17,1},{2,18},{18,2},{3,19},{19,3},{4,20},{20... | collective-permute-start | bytes 1474568 | tf_op jit(solution)/shard_map/ppermute | solution.py:23
  178.7 23.4 %collective-permute-start.14 = (bf16[160,1536]{1,0:T(8,128)(2,1)}, bf16[160,1536]{1,0:T(8,128)(2,1)}, u32[]{:S(2)}, u32[]{:S(2)}) collective-permute-start(bf16[160,1536]{1,0:T(8,128)(2,1)} %get-tuple-element.26), channel_id=1, source_target_pairs={{0,16},{16,0},{1,17},{17,1},{2,18},{18,2},{3,19},{19,3},{4,20},{20... | collective-permute-start | bytes 1474568 | tf_op jit(solution)/shard_map/ppermute | solution.py:23
  179.2 33.4 %collective-permute-start.16 = (bf16[160,1536]{1,0:T(8,128)(2,1)}, bf16[160,1536]{1,0:T(8,128)(2,1)}, u32[]{:S(2)}, u32[]{:S(2)}) collective-permute-start(bf16[160,1536]{1,0:T(8,128)(2,1)} %get-tuple-element.22), channel_id=1, source_target_pairs={{0,16},{16,0},{1,17},{17,1},{2,18},{18,2},{3,19},{19,3},{4,20},{20... | collective-permute-start | bytes 1474568 | tf_op jit(solution)/shard_map/ppermute | solution.py:23
  180.7 41.7 %collective-permute-start.15 = (bf16[160,1536]{1,0:T(8,128)(2,1)}, bf16[160,1536]{1,0:T(8,128)(2,1)}, u32[]{:S(2)}, u32[]{:S(2)}) collective-permute-start(bf16[160,1536]{1,0:T(8,128)(2,1)} %get-tuple-element.24), channel_id=1, source_target_pairs={{0,16},{16,0},{1,17},{17,1},{2,18},{18,2},{3,19},{19,3},{4,20},{20... | collective-permute-start | bytes 1474568 | tf_op jit(solution)/shard_map/ppermute | solution.py:23
  357.5 19.9 %collective-permute-start.17 = (bf16[320,768]{1,0:T(8,128)(2,1)S(1)}, bf16[320,768]{1,0:T(8,128)(2,1)S(1)}, u32[]{:S(2)}, u32[]{:S(2)}) collective-permute-start(bf16[320,768]{1,0:T(8,128)(2,1)S(1)} %bitcast.123), channel_id=1, source_target_pairs={{0,16},{16,0},{1,17},{17,1},{2,18},{18,2},{3,19},{19,3},{4,20},{20... | collective-permute-start | bytes 1474568 | tf_op jit(solution)/shard_map/ppermute | solution.py:23
  361.2 21.0 %collective-permute-start.18 = (bf16[320,768]{1,0:T(8,128)(2,1)S(1)}, bf16[320,768]{1,0:T(8,128)(2,1)S(1)}, u32[]{:S(2)}, u32[]{:S(2)}) collective-permute-start(bf16[320,768]{1,0:T(8,128)(2,1)S(1)} %bitcast.122), channel_id=1, source_target_pairs={{0,16},{16,0},{1,17},{17,1},{2,18},{18,2},{3,19},{19,3},{4,20},{20... | collective-permute-start | bytes 1474568 | tf_op jit(solution)/shard_map/ppermute | solution.py:23
  364.3 28.3 %collective-permute-start.19 = (bf16[320,768]{1,0:T(8,128)(2,1)S(1)}, bf16[320,768]{1,0:T(8,128)(2,1)S(1)}, u32[]{:S(2)}, u32[]{:S(2)}) collective-permute-start(bf16[320,768]{1,0:T(8,128)(2,1)S(1)} %bitcast.121), channel_id=1, source_target_pairs={{0,16},{16,0},{1,17},{17,1},{2,18},{18,2},{3,19},{19,3},{4,20},{20... | collective-permute-start | bytes 1474568 | tf_op jit(solution)/shard_map/ppermute | solution.py:23
  367.7 34.9 %collective-permute-start.20 = (bf16[320,768]{1,0:T(8,128)(2,1)S(1)}, bf16[320,768]{1,0:T(8,128)(2,1)S(1)}, u32[]{:S(2)}, u32[]{:S(2)}) collective-permute-start(bf16[320,768]{1,0:T(8,128)(2,1)S(1)} %bitcast.120), channel_id=1, source_target_pairs={{0,16},{16,0},{1,17},{17,1},{2,18},{18,2},{3,19},{19,3},{4,20},{20... | collective-permute-start | bytes 1474568 | tf_op jit(solution)/shard_map/ppermute | solution.py:23
  382.7 20.4 %copy-start.28 = (bf16[4,80,2048]{2,1,0:T(8,128)(2,1)S(1)}, bf16[4,80,2048]{2,1,0:T(8,128)(2,1)}, u32[]{:S(2)}) copy-start(bf16[4,80,2048]{2,1,0:T(8,128)(2,1)} %copy-done.27) | copy-start | bytes 3932164
  382.7 20.4 %copy-start.30 = (bf16[4,80,2048]{2,1,0:T(8,128)(2,1)S(1)}, bf16[4,80,2048]{2,1,0:T(8,128)(2,1)}, u32[]{:S(2)}) copy-start(bf16[4,80,2048]{2,1,0:T(8,128)(2,1)} %copy-done.29) | copy-start | bytes 3932164
  (28 other events, 158.6 us)
Sparse Core Ops, SparseCore 0:
  10.2 77.6 all-gather.2
  177.2 86.3 reduce-scatter.1
  278.0 74.6 all-gather.4
